TPU v7x, 32 devices: a whole 2x2x4 slice. The times are simulated.
32 devices in a mesh: band: 16 (over z, y, x), disp: 2 (over core).
Axes of the slice: x: 2, y: 2, z: 4, core: 2. Of those that a mesh axis runs over, the one named last changes fastest.
Arguments:
- feat_left: bfloat16 [16, 96, 256], P('band', None, 'disp'), may hold values from -19 to 19
- feat_right: bfloat16 [16, 96, 256], P('band', None, 'disp'), may hold values from -19 to 19
- limit: int32 [16, 256], P('band', 'disp'), may hold values from 24 to 96
- indices: int32 [3, 16, 256], P(None, 'band', 'disp'), may hold values from 0 to 95
- hidden_start: bfloat16 [16, 256, 128], P('band', 'disp'), may hold values from -1 to 1
- vol_kernel: bfloat16 [3, 3, 3, 8, 8], replicated, may hold values from -0.4375 to 0.4375
- group_gain: float32 [8], replicated, may hold values from 0.5 to 2
- hid_kernel: bfloat16 [3, 3, 128, 384], replicated, may hold values from -0.1875 to 0.1875
- in_kernel: bfloat16 [3, 3, 9, 384], replicated, may hold values from -0.625 to 0.625
- head_weight: bfloat16 [128, 1], replicated, may hold values from -0.5 to 0.5
Outputs:
- disparity: float32 [16, 256], P('band', 'disp')
- hidden: bfloat16 [16, 256, 128], P('band', 'disp')
All inputs are finite; a program needn't handle non-finite values.
Results may differ from a plain program's by a relative error of at most 0.007.
Values may be sent and summed in bfloat16 or wider, within the bound.
No kernel may reach another device: no remote copies, remote signals or barrier semaphores. Data moves between devices by JAX's collectives and lax.ppermute only.
A program may use at most 128 MiB of HBM per device.

v0:
```python
import jax
import jax.numpy as jnp
from jax import lax
from jax.experimental import pallas as pl
from jax.experimental.pallas import tpu as pltpu
from jax.sharding import PartitionSpec as P

GROUPS = 8
DISPS = 96
FEAT_CH = 96
HID_CH = 128
ITERS = 3
TILE = 128
REACH = 2 * ITERS
EDGE = 8
QUAD = 4
STRIP = TILE // QUAD
WINDOW = STRIP + 2 * EDGE
PACK = 32
PITCH = 64
ORDER = (0, 3, 1, 2)
BLOCK_ROWS = WINDOW + 2 * GROUPS
AROUND = QUAD + 2 * REACH
BLOCK = 8
SLAB = (BLOCK + 2) * GROUPS
OUT_SLAB = BLOCK * GROUPS

pixel_unit = 8.0
feature_scale = 0.25
floor_logit = -1e30

f32 = jnp.float32
bf16 = jnp.bfloat16


def dot(a, b):
    return jnp.dot(a, b, preferred_element_type=f32)


def dot_nt(a, b):
    return lax.dot_general(a, b, (((1,), (1,)), ((), ())), preferred_element_type=f32)


def copy_all(copies):
    for copy in copies:
        copy.start()
    for copy in copies:
        copy.wait()


def toeplitz(vol_kernel):
    size = 27 * GROUPS
    flat = vol_kernel[...].astype(f32).reshape(size, GROUPS)
    flat = jnp.concatenate([flat, jnp.zeros((size, TILE - GROUPS), f32)], axis=1).T[:GROUPS]
    row = lax.broadcasted_iota(jnp.int32, (9 * GROUPS, size), 0) >> 3
    tap = lax.broadcasted_iota(jnp.int32, (9 * GROUPS, size), 1) >> 3
    tap_a = (tap >= 9).astype(jnp.int32) + (tap >= 18).astype(jnp.int32)
    within = tap - 9 * tap_a
    tap_b = (within >= 3).astype(jnp.int32) + (within >= 6).astype(jnp.int32)
    tap_e = within - 3 * tap_b
    pairs = jnp.where(
        row == 3 * tap_a + tap_e, jnp.concatenate([flat] * 9, axis=0), 0.0
    ).astype(bf16)
    from_row = lax.broadcasted_iota(jnp.int32, (size, 3 * SLAB), 0)
    to = lax.broadcasted_iota(jnp.int32, (size, 3 * SLAB), 1)
    from_tap = from_row >> 3
    from_in = from_tap - 9 * ((from_tap >= 9).astype(jnp.int32) + (from_tap >= 18).astype(jnp.int32))
    from_b = (from_in >= 3).astype(jnp.int32) + (from_in >= 6).astype(jnp.int32)
    to_b = (to >= SLAB).astype(jnp.int32) + (to >= 2 * SLAB).astype(jnp.int32)
    repeat = jnp.where((from_b == to_b) & ((from_row & 7) == (to & 7)), 1.0, 0.0).astype(bf16)
    spread = dot(pairs, repeat)
    to = lax.broadcasted_iota(jnp.int32, (GROUPS, 3 * SLAB), 1)
    to_b = (to >= SLAB).astype(jnp.int32) + (to >= 2 * SLAB).astype(jnp.int32)
    to_d = (to - SLAB * to_b) >> 3
    rows = []
    for e in range(3):
        for d in range(BLOCK):
            value = jnp.zeros((GROUPS, 3 * SLAB), f32)
            for a in range(3):
                at = (3 * a + e) * GROUPS
                value = jnp.where(to_d == d + a, spread[at : at + GROUPS], value)
            rows.append(value)
    return jnp.concatenate(rows, axis=0).astype(bf16)


def interleaved(values):
    stacked = jnp.swapaxes(jnp.stack(values), 0, 1)
    return stacked.reshape(values[0].shape[0] * len(values), values[0].shape[1])


def correlate(lefts, rights, place, row_ok, wide, extra):
    has_left = (place[1] > 0).astype(f32)
    has_right = (place[1] < place[3] - 1).astype(f32)
    lane = lax.broadcasted_iota(jnp.int32, (TILE, TILE), 1)
    sub = lax.broadcasted_iota(jnp.int32, (TILE, TILE), 0)
    flip = jnp.where(lane + sub == TILE - 1, 1.0, 0.0).astype(bf16)
    per_group = FEAT_CH // GROUPS
    channel = lax.broadcasted_iota(jnp.int32, (32, FEAT_CH), 1)
    group_masks = [
        (channel >= g * per_group) & (channel < (g + 1) * per_group) for g in range(GROUPS)
    ]
    lane96 = lax.broadcasted_iota(jnp.int32, (FEAT_CH, TILE), 1)
    zero_slab = jnp.zeros((GROUPS, TILE), f32)
    for at in (0, (DISPS + 1) * GROUPS):
        wide[pl.ds(at, GROUPS), :] = zero_slab
        extra[pl.ds(at, GROUPS), :] = zero_slab

    own_t = (lefts[1] * row_ok).T
    side_t = jnp.where(
        lane96 < EDGE,
        lefts[2] * (has_right * row_ok),
        jnp.where(lane96 >= TILE - EDGE, lefts[0] * (has_left * row_ok), 0.0),
    ).T
    sources = jnp.concatenate([rights[2] * has_right, rights[1], rights[0] * has_left], axis=0)
    flipped = dot(sources.astype(bf16), flip)
    reverse = jnp.concatenate(
        [flipped[i * FEAT_CH : (i + 1) * FEAT_CH] for i in range(3)], axis=1
    )
    windows = [
        reverse[:, 2 * TILE - 32 - 32 * k : 3 * TILE - 32 - 32 * k].astype(bf16)
        for k in range(-1, 5)
    ]

    def by_group(rows):
        count = rows.shape[0]
        parts = [jnp.where(m[:count], rows, 0.0) for m in group_masks]
        return jnp.concatenate(parts, axis=0).astype(bf16)

    def shear(product, g, count, first):
        rows = product[count * g : count * g + count]
        return pltpu.roll(rows, TILE - 31 + first, 1, stride=1, stride_axis=0)

    products = [
        dot(by_group(own_t[32 * k : 32 * k + 32]), windows[k + 1]) for k in range(TILE // 32)
    ]
    after = dot(by_group(side_t[:EDGE]), windows[5])
    before = dot(by_group(side_t[TILE - EDGE :]), windows[0])
    parts, sides = [], []
    for g in range(GROUPS):
        part = jnp.concatenate([shear(product, g, 32, 0) for product in products], axis=0)
        parts.append(part.T[:DISPS])
        sides += [shear(after, g, EDGE, 0), shear(before, g, EDGE, 32 - EDGE)]
    part = jnp.concatenate(sides, axis=0).T[:DISPS]
    sides = [part if g == 0 else pltpu.roll(part, TILE - 2 * EDGE * g, 1) for g in range(GROUPS)]
    for target, values in ((wide, parts), (extra, sides)):
        target[GROUPS : GROUPS + DISPS * GROUPS, :] = interleaved(values) * (1.0 / per_group)


def own_row_kernel(
    place, own, across, limit, indices, vol_kernel, raw_out, taps_out, marks_out, wide, extra,
    kernel, sem,
):
    copy = pltpu.make_async_copy(vol_kernel, kernel, sem.at[0])
    copy.start()
    tiles = [across[0], own[...], across[across.shape[0] - 1]]
    tiles = [tile.astype(f32) for tile in tiles]
    correlate(
        [tile[:FEAT_CH] for tile in tiles], [tile[FEAT_CH:] for tile in tiles],
        place, 1.0, wide, extra,
    )
    raw_out[...] = jnp.concatenate([wide[...], extra[...]], axis=1).astype(bf16)
    marks = [limit[...]] + [indices[t] for t in range(ITERS)]
    blank = jnp.zeros((GROUPS - len(marks), TILE), jnp.int32)
    marks_out[...] = jnp.concatenate(marks + [blank], axis=0)
    copy.wait()
    taps_out[...] = toeplitz(kernel)


def volume_kernel(
    place, gain, odd_own, odd_across, even_own, even_across, marks, marks_across, hidden,
    hidden_across, raw_own, taps_own, out_0, out_1, out_2, out_3, raw, taps, wide, extra, logit, padded, blocks, sems,
):
    band, bands = place[0], place[2]
    is_even = band % 2 == 0
    copies = [
        pltpu.make_async_copy(raw_own, raw, sems.at[0]),
        pltpu.make_async_copy(taps_own, taps, sems.at[1]),
    ]
    for copy in copies:
        copy.start()

    last = odd_across.shape[0] - 1
    odd = [tile.astype(f32) for tile in (odd_across[0], odd_own[...], odd_across[last])]
    even = [tile.astype(f32) for tile in (even_across[0], even_own[...], even_across[last])]
    for b in range(2):
        row = band + 2 * b - 1
        row_ok = ((row >= 0) & (row < bands)).astype(f32)
        tiles = [
            jnp.where(is_even, y, x) if b == 0 else jnp.where(is_even, x, y)
            for x, y in zip(odd, even)
        ]
        correlate(
            [tile[:FEAT_CH] for tile in tiles], [tile[FEAT_CH:] for tile in tiles],
            place, row_ok, wide.at[b], extra.at[b],
        )
    for copy in copies:
        copy.wait()

    lane = lax.broadcasted_iota(jnp.int32, (GROUPS, TILE), 1)
    left_marks = pltpu.roll(marks_across[0], 2 * EDGE, 1)
    levels_of = [marks[...], jnp.where(lane < EDGE, marks_across[last], left_marks)]
    lane8 = lax.broadcasted_iota(jnp.int32, (OUT_SLAB, TILE), 1)
    group_at = lax.broadcasted_iota(jnp.int32, (GROUPS, TILE), 0)
    gains = jnp.zeros((GROUPS, TILE), f32)
    for g in range(GROUPS):
        gains = jnp.where(group_at == g, gain[g], gains)
    wanted = [
        [jnp.broadcast_to(rows[t + 1 : t + 2], (GROUPS, TILE)) for t in range(ITERS)]
        for rows in levels_of
    ]
    found = [[jnp.zeros((GROUPS, TILE), f32) for _ in range(ITERS)] for _ in range(2)]
    for q in range(DISPS // BLOCK):
        at = q * OUT_SLAB
        slabs = [
            jnp.concatenate(
                [wide[b, at : at + SLAB, :], extra[b, at : at + SLAB, :]], axis=1
            ).astype(bf16)
            for b in range(2)
        ]
        slabs.insert(1, raw[at : at + SLAB, :])
        product = dot(taps[...], jnp.concatenate(slabs, axis=0))
        halves = [product[:, :TILE], product[:, TILE:]]
        first = [half[:OUT_SLAB] for half in halves]
        middle = [half[OUT_SLAB : 2 * OUT_SLAB] for half in halves]
        after = [half[2 * OUT_SLAB :] for half in halves]
        first_on = pltpu.roll(first[0], 1, 1)
        convs = [
            middle[0]
            + jnp.where(lane8 == 0, pltpu.roll(first[1], TILE - 2 * EDGE + 1, 1), first_on)
            + jnp.where(
                lane8 == TILE - 1,
                pltpu.roll(after[1], TILE - 1, 1),
                pltpu.roll(after[0], TILE - 1, 1),
            ),
            middle[1]
            + jnp.where(lane8 == 0, first_on, pltpu.roll(first[1], 1, 1))
            + jnp.where(
                lane8 == 2 * EDGE - 1,
                pltpu.roll(after[0], 2 * EDGE - 1, 1),
                pltpu.roll(after[1], TILE - 1, 1),
            ),
        ]
        centre = slabs[1].astype(f32)[GROUPS : GROUPS + OUT_SLAB]
        for i in range(2):
            volume = centre[:, i * TILE : (i + 1) * TILE] + jnp.maximum(convs[i], 0.0)
            volume = volume.astype(bf16).astype(f32).reshape(BLOCK, GROUPS, TILE)
            logit[i, q * BLOCK : (q + 1) * BLOCK, :] = jnp.sum(volume * gains[None], axis=1)
            for d in range(BLOCK):
                for t in range(ITERS):
                    hit = wanted[i][t] == q * BLOCK + d
                    found[i][t] = found[i][t] + jnp.where(hit, volume[d], 0.0)

    level = lax.broadcasted_iota(jnp.int32, (DISPS, TILE), 0)
    for i in range(2):
        valid = level < levels_of[i][0:1]
        masked = jnp.where(valid, logit[i], floor_logit)
        top = jnp.max(masked, axis=0, keepdims=True)
        weights = jnp.where(valid, jnp.exp(masked - top), 0.0)
        moment = jnp.sum(weights * level.astype(f32), axis=0, keepdims=True)
        start = moment / jnp.sum(weights, axis=0, keepdims=True) / pixel_unit
        high = start.astype(bf16).astype(f32)
        low = (start - high).astype(bf16).astype(f32)
        ends = jnp.where(
            group_at == 0,
            jnp.broadcast_to(high, (GROUPS, TILE)),
            jnp.where(group_at == 1, jnp.broadcast_to(low, (GROUPS, TILE)), 0.0),
        )
        found[i].append(ends)
    has_left, has_right = place[1] > 0, place[1] < place[3] - 1
    is_beside = ((lane < EDGE) & has_right) | ((lane >= EDGE) & (lane < 2 * EDGE) & has_left)
    packed, packed_beside = found[0], [jnp.where(is_beside, x, 0.0) for x in found[1]]

    before = hidden_across[0, TILE - 2 * EDGE :, :].astype(f32)[EDGE:]
    after = hidden_across[last, : 2 * EDGE, :].astype(f32)[:EDGE]
    padded[:EDGE, :] = jnp.where(has_left, before, 0.0)
    padded[EDGE : EDGE + TILE, :] = hidden[...].astype(f32)
    padded[EDGE + TILE :, :] = jnp.where(has_right, after, 0.0)
    for strip in range(QUAD):
        block = [padded[STRIP * strip : STRIP * strip + WINDOW, :]]
        for half in range(2):
            part = jnp.zeros((GROUPS, TILE), f32)
            for i in range(2):
                q, base = 2 * half + i, PITCH * i
                at = lane - base
                moved = pltpu.roll(packed[q], (base + EDGE - STRIP * strip) % TILE, 1)
                if strip == 0:
                    other = pltpu.roll(packed_beside[q], (base - EDGE) % TILE, 1)
                    moved = jnp.where(at < EDGE, other, moved)
                if strip == QUAD - 1:
                    other = pltpu.roll(packed_beside[q], base + WINDOW - EDGE, 1)
                    moved = jnp.where(at >= WINDOW - EDGE, other, moved)
                part = jnp.where((at >= 0) & (at < WINDOW), moved, part)
            block.append(part)
        blocks[strip] = jnp.concatenate(block, axis=0).astype(bf16)
    member = band % QUAD
    for i, out in zip(ORDER, (out_0, out_1, out_2, out_3)):
        out[...] = blocks[strip_at(place, member ^ i)]


def slot_of(member_xor):
    return jnp.where(member_xor == 0, 0, jnp.where(member_xor == 3, 1, member_xor + 1))


def strip_at(place, member):
    return jnp.where(place[1] % 2 == 0, member, QUAD - 1 - member)


def keep(line, target, at, values):
    length = values.shape[0]
    start = EDGE + at
    line[start : start + length, :] = values
    target[at : at + length, 0:HID_CH] = line[start - 1 : start - 1 + length, :].astype(bf16)
    target[at : at + length, HID_CH : 2 * HID_CH] = values.astype(bf16)
    target[at : at + length, 2 * HID_CH :] = line[start + 1 : start + 1 + length, :].astype(bf16)


def around(target, at, length):
    return [target[at + a * WINDOW : at + a * WINDOW + length, :] for a in (-1, 0, 1)]


def refine_kernel(
    place,
    own,
    far_c,
    far_d,
    near_a,
    near_b,
    hid_weight,
    in_weight,
    head,
    out_0,
    out_1,
    out_2,
    out_3,
    line,
    weight,
    looked,
    hidden_at,
    taps,
    reset_taps,
    inputs,
    gate,
    level,
    blocks,
    sems,
):
    rows, strip = AROUND, STRIP
    copies = [
        pltpu.make_async_copy(hid_weight, weight.at[pl.ds(0, 9 * HID_CH)], sems.at[0])
    ]
    copies.append(
        pltpu.make_async_copy(
            in_weight, weight.at[pl.ds(9 * HID_CH, 3 * HID_CH)], sems.at[1]
        )
    )
    for copy in copies:
        copy.start()

    band, disp, bands, disps = place[0], place[1], place[2], place[3]
    member, layer = band % QUAD, band // QUAD
    at = strip_at(place, member)
    first = strip * at - EDGE
    first_row = layer * QUAD - REACH

    def block_of(r):
        step, row = (r + 2 * QUAD - REACH) // QUAD - 2, (r + 2 * QUAD - REACH) % QUAD
        slot = slot_of(row ^ member)
        if step == 0:
            return own[slot].astype(f32)
        if abs(step) == 1:
            choice, x, y = (layer % 2 == 0) == (step > 0), near_a, near_b
        else:
            choice, x, y = (layer % 4 < 2) == (step > 0), far_c, far_d
        inside = (first_row + r >= 0) & (first_row + r < bands)
        block = jnp.where(choice, x[slot].astype(f32), y[slot].astype(f32))
        return jnp.where(inside, block, 0.0)

    lane = lax.broadcasted_iota(jnp.int32, (GROUPS, TILE), 1)
    at_sub = lax.broadcasted_iota(jnp.int32, (WINDOW, TILE), 0)
    at_lane = lax.broadcasted_iota(jnp.int32, (WINDOW, TILE), 1)
    spread = jnp.where(at_sub == at_lane % PITCH, 1.0, 0.0).astype(bf16)
    fill = jnp.zeros((PACK, TILE), f32)
    zeros = jnp.zeros((GROUPS, TILE), f32)
    lines = []
    for r in range(rows):
        block = block_of(r)
        packed = block[WINDOW:]
        hidden_at[r * WINDOW : (r + 1) * WINDOW, :] = block[:WINDOW]
        pieces = []
        for b in range(3):
            moved = packed if b == 1 else pltpu.roll(packed, (1 - b) % TILE, 1)
            for q in range(4):
                part = moved[GROUPS * (q // 2) : GROUPS * (q // 2 + 1)]
                pieces.append(jnp.where((lane >= PITCH) == (q % 2 == 1), part, zeros))
        lines.append(jnp.concatenate(pieces + [fill], axis=0).astype(bf16))
    for r in range(0, rows, 2):
        both = dot_nt(spread, jnp.concatenate(lines[r : r + 2], axis=0))
        for i in range(2):
            at = (r + i) * WINDOW
            looked[at : at + WINDOW, :] = both[:, i * HID_CH : (i + 1) * HID_CH]
    sub = lax.broadcasted_iota(jnp.int32, (HID_CH, HID_CH), 0)
    ends = jnp.where((sub == PACK + 24) | (sub == PACK + 25), feature_scale, 0.0).astype(bf16)
    blank = jnp.zeros((EDGE, HID_CH), f32)
    level[:EDGE, :] = blank
    level[EDGE + WINDOW * rows :, :] = blank
    level[EDGE : EDGE + WINDOW * rows, :] = dot(looked[...].astype(bf16), ends)
    line[...] = jnp.zeros_like(line)
    keep(line, taps, 0, hidden_at[...])
    for copy in copies:
        copy.wait()
    heads = jnp.broadcast_to(head[...].astype(f32) * feature_scale, (HID_CH, HID_CH)).astype(bf16)

    for t in range(ITERS):
        low, high = 1 + 2 * t, rows - 2 - 2 * t
        at, length = (low - 1) * WINDOW, (high - low + 3) * WINDOW
        lane_at = lax.broadcasted_iota(jnp.int32, (length, HID_CH), 1)
        tap, channel = lane_at // PACK, lane_at % PACK
        near = [level[EDGE + at + b : EDGE + at + b + length, :] for b in (-1, 0, 1)]
        value = jnp.where(tap == 0, near[0], jnp.where(tap == 1, near[1], near[2]))
        at_lookup = (channel >= t * GROUPS) & (channel < (t + 1) * GROUPS)
        value = jnp.where(
            (channel == 3 * GROUPS) & (tap < 3),
            value,
            jnp.where(at_lookup, looked[at : at + length, :], 0.0),
        )
        inputs[at : at + length, :] = value.astype(bf16)

        at, length = low * WINDOW, (high - low + 1) * WINDOW
        lhs = around(taps, at, length) + around(inputs, at, length)
        both = dot(jnp.concatenate(lhs, axis=1), weight[:, : 2 * HID_CH])
        gate[at + WINDOW : at + length - WINDOW, :] = (
            0.5 * jnp.tanh(0.5 * both[WINDOW : length - WINDOW, :HID_CH]) + 0.5
        )
        reset = 0.5 * jnp.tanh(0.5 * both[:, HID_CH:]) + 0.5
        keep(line, reset_taps, at, reset * hidden_at[at : at + length, :])

        at, length = at + WINDOW, length - 2 * WINDOW
        lhs = around(reset_taps, at, length) + around(inputs, at, length)
        candidate = jnp.tanh(dot(jnp.concatenate(lhs, axis=1), weight[:, 2 * HID_CH :]))
        hidden = hidden_at[at : at + length, :]
        hidden = hidden + gate[at : at + length, :] * (candidate - hidden)
        pixel = lax.broadcasted_iota(jnp.int32, (length, HID_CH), 0)
        column, row = pixel % WINDOW + first, pixel // WINDOW + (low + 1 + first_row)
        inside = ((column >= 0) | (disp > 0)) & ((column < TILE) | (disp < disps - 1))
        inside = inside & (row >= 0) & (row < bands)
        hidden = jnp.where(inside, hidden, 0.0).astype(bf16)
        level[EDGE + at : EDGE + at + length, :] += dot_nt(hidden, heads)
        hidden_at[at : at + length, :] = hidden.astype(f32)
        if t < ITERS - 1:
            keep(line, taps, at, hidden.astype(f32))

    lane = lax.broadcasted_iota(jnp.int32, (strip, HID_CH), 1)
    for r in range(QUAD):
        at = (REACH + r) * WINDOW + EDGE
        hidden = hidden_at[at : at + strip, :]
        value = level[EDGE + at : EDGE + at + strip, :] * (1.0 / feature_scale)
        high = value.astype(bf16).astype(f32)
        middle = (value - high).astype(bf16).astype(f32)
        parts = jnp.where(lane == 0, high, jnp.where(lane == 1, middle, value - high - middle))
        parts = jnp.where(lane < 3, parts, 0.0)
        blocks[r] = jnp.concatenate([hidden, parts], axis=0).astype(bf16)
    for i, out in zip(ORDER, (out_0, out_1, out_2, out_3)):
        out[...] = blocks[member ^ i]


def unpack_kernel(place, from_0, from_1, from_2, from_3, disparity_out, hidden_out, blocks):
    for i, block in enumerate((from_0, from_1, from_2, from_3)):
        blocks[i] = block[...]
    member = place[0] % QUAD
    slots = [slot_of(strip_at(place, strip) ^ member) for strip in range(QUAD)]
    held = [blocks[slot].astype(f32) for slot in slots]
    hidden_out[0] = jnp.concatenate([block[:STRIP] for block in held], axis=0).astype(bf16)
    parts = jnp.concatenate([block[STRIP:] for block in held], axis=0).T
    disparity_out[...] = parts[0:1] + parts[1:2] + parts[2:3]


def in_hbm(value):
    return pltpu.with_memory_space_constraint(value, pltpu.HBM)


def to_sides(value):
    disps = lax.axis_size("disp")
    right = [(d, d + 1) for d in range(disps - 1)]
    left = [(d + 1, d) for d in range(disps - 1)]
    if disps == 2:
        return lax.ppermute(value, "disp", right + left)[None]
    return jnp.stack([lax.ppermute(value, "disp", right), lax.ppermute(value, "disp", left)])


def in_group(blocks):
    return [blocks[0]] + [
        to_rows(block, lambda band, i=i: band ^ i)
        for i, block in list(zip(ORDER, blocks))[1:]
    ]


def to_layers(value, partner):
    groups = lax.axis_size("band") // QUAD
    if not any(0 <= partner(g) < groups for g in range(groups)):
        return None
    return to_rows(value, lambda band: partner(band // QUAD) * QUAD + band % QUAD)


def to_rows(value, shift):
    bands = lax.axis_size("band")
    return lax.ppermute(
        value, "band", [(i, shift(i)) for i in range(bands) if 0 <= shift(i) < bands]
    )


def odd_pair(i):
    return i ^ 1


def even_pair(i):
    return i - 1 if i % 2 == 0 else i + 1


def local(
    feat_left,
    feat_right,
    limit,
    indices,
    hidden_start,
    vol_kernel,
    group_gain,
    hid_kernel,
    in_kernel,
    head_weight,
):
    bands, disps = lax.axis_size("band"), lax.axis_size("disp")
    place = jnp.stack(
        [lax.axis_index("band"), lax.axis_index("disp"), jnp.int32(bands), jnp.int32(disps)]
    ).astype(jnp.int32)
    smem = pl.BlockSpec(memory_space=pltpu.SMEM)
    vmem = pl.BlockSpec(memory_space=pltpu.VMEM)
    hbm = pl.BlockSpec(memory_space=pltpu.HBM)
    anywhere = pl.BlockSpec(memory_space=pl.ANY)
    padded = (DISPS + 2) * GROUPS

    feats = jnp.concatenate([feat_left[0], feat_right[0]], axis=0)
    odd_own, even_own = to_rows(feats, odd_pair), to_rows(feats, even_pair)
    across = to_sides(feats)
    raw_own, taps, marks = pl.pallas_call(
        own_row_kernel,
        out_shape=(
            jax.ShapeDtypeStruct((padded, 2 * TILE), bf16),
            jax.ShapeDtypeStruct((3 * OUT_SLAB, 3 * SLAB), bf16),
            jax.ShapeDtypeStruct((GROUPS, TILE), jnp.int32),
        ),
        in_specs=[smem, vmem, vmem, vmem, vmem, hbm],
        out_specs=(vmem, vmem, vmem),
        scratch_shapes=[
            pltpu.VMEM((padded, TILE), f32),
            pltpu.VMEM((padded, TILE), f32),
            pltpu.VMEM((27, GROUPS, GROUPS), bf16),
            pltpu.SemaphoreType.DMA((1,)),
        ],
        compiler_params=pltpu.CompilerParams(vmem_limit_bytes=16 * 2**20),
        cost_estimate=pl.CostEstimate(flops=2 * 10**9, bytes_accessed=4 * 2**20, transcendentals=0),
    )(
        place, feats, across, in_hbm(limit), in_hbm(indices),
        in_hbm(vol_kernel.reshape(27, GROUPS, GROUPS)),
    )
    hidden = hidden_start[0]
    hidden_across = to_sides(hidden)
    odd_own, even_own, raw_own, taps, hidden_across = lax.optimization_barrier(
        (odd_own, even_own, raw_own, taps, hidden_across)
    )
    marks_across = to_sides(marks)
    odd_across, even_across = to_sides(odd_own), to_sides(even_own)

    in_weight = jnp.concatenate(
        [in_kernel[:, :, :GROUPS]] * ITERS + [in_kernel[:, :, GROUPS:]], axis=2
    )
    in_weight = jnp.pad(in_weight, ((0, 0), (0, 1), (0, PACK - in_weight.shape[2]), (0, 0)))
    in_weight = in_weight.reshape(3 * HID_CH, 3 * HID_CH)

    blocks = pl.pallas_call(
        volume_kernel,
        out_shape=(jax.ShapeDtypeStruct((BLOCK_ROWS, TILE), bf16),) * QUAD,
        in_specs=[smem, smem] + [vmem] * 8 + [hbm, hbm],
        out_specs=(vmem,) * QUAD,
        scratch_shapes=[
            pltpu.VMEM((padded, 2 * TILE), bf16),
            pltpu.VMEM((3 * OUT_SLAB, 3 * SLAB), bf16),
            pltpu.VMEM((2, padded, TILE), f32),
            pltpu.VMEM((2, padded, TILE), f32),
            pltpu.VMEM((2, DISPS, TILE), f32),
            pltpu.VMEM((TILE + 2 * EDGE, HID_CH), f32),
            pltpu.VMEM((QUAD, BLOCK_ROWS, TILE), bf16),
            pltpu.SemaphoreType.DMA((2,)),
        ],
        compiler_params=pltpu.CompilerParams(vmem_limit_bytes=24 * 2**20),
        cost_estimate=pl.CostEstimate(
            flops=5 * 10**9, bytes_accessed=16 * 2**20, transcendentals=DISPS * TILE
        ),
    )(
        place, in_hbm(group_gain), odd_own, odd_across, even_own, even_across,
        marks, marks_across, in_hbm(hidden), hidden_across, raw_own, taps,
    )

    own, in_weight = lax.optimization_barrier((jnp.stack(in_group(blocks)), in_weight))
    around = [
        to_layers(own, lambda g: g ^ 2),
        to_layers(own, lambda g: (g - 2 ^ 2) + 2),
        to_layers(own, lambda g: g ^ 1),
        to_layers(own, lambda g: (g - 1 ^ 1) + 1),
    ]
    if around[1] is None:
        around[1] = around[0]

    pixels = WINDOW * AROUND
    refined = pl.pallas_call(
        refine_kernel,
        out_shape=(jax.ShapeDtypeStruct((2 * STRIP, HID_CH), bf16),) * QUAD,
        in_specs=[smem] + [vmem] * 5 + [anywhere, anywhere, vmem],
        out_specs=(vmem,) * QUAD,
        scratch_shapes=[
            pltpu.VMEM((pixels + 2 * EDGE, HID_CH), f32),
            pltpu.VMEM((12 * HID_CH, 3 * HID_CH), bf16),
            pltpu.VMEM((pixels, HID_CH), f32),
            pltpu.VMEM((pixels, HID_CH), f32),
            pltpu.VMEM((pixels, 3 * HID_CH), bf16),
            pltpu.VMEM((pixels, 3 * HID_CH), bf16),
            pltpu.VMEM((pixels, HID_CH), bf16),
            pltpu.VMEM((pixels, HID_CH), f32),
            pltpu.VMEM((pixels + 2 * EDGE, HID_CH), f32),
            pltpu.VMEM((QUAD, 2 * STRIP, HID_CH), bf16),
            pltpu.SemaphoreType.DMA((2,)),
        ],
        compiler_params=pltpu.CompilerParams(vmem_limit_bytes=32 * 2**20),
    )(
        place, own, *around,
        hid_kernel.reshape(9 * HID_CH, 3 * HID_CH), in_weight,
        in_hbm(head_weight.reshape(1, HID_CH)),
    )
    disparity, hidden = pl.pallas_call(
        unpack_kernel,
        out_shape=(
            jax.ShapeDtypeStruct((1, TILE), f32),
            jax.ShapeDtypeStruct((1, TILE, HID_CH), bf16),
        ),
        in_specs=[smem] + [vmem] * QUAD,
        out_specs=(vmem, vmem),
        scratch_shapes=[pltpu.VMEM((QUAD, 2 * STRIP, HID_CH), bf16)],
        compiler_params=pltpu.CompilerParams(vmem_limit_bytes=4 * 2**20),
    )(place, *in_group(refined))
    return (disparity, hidden)


def solution(mesh):
    in_specs = (
        P("band", None, "disp"),
        P("band", None, "disp"),
        P("band", "disp"),
        P(None, "band", "disp"),
        P("band", "disp", None),
        P(),
        P(),
        P(),
        P(),
        P(),
    )
    out_specs = (P("band", "disp"), P("band", "disp", None))
    return jax.shard_map(local, mesh=mesh, in_specs=in_specs, out_specs=out_specs, check_vma=False)
```

profile of v0, /device:TPU:8, one launch (start us, length us, event | category | flops | bytes accessed | tf_op | source)
XLA Modules:
  0.0 46.0 jit_solution(9682310451497653746)
XLA Ops:
  0.6 0.0 copy-start.2
  0.6 0.8 %pad_maximum_fusion.2.own = bf16[192,128]{1,0:T(8,128)(2,1)S(1)} fusion(bf16[96,128]{1,0:T(8,128)(2,1)} %bitcast.26, bf16[96,128]{1,0:T(8,128)(2,1)} %bitcast.27), kind=kLoop, calls=%fused_computation.2 | loop fusion | flops 98304 | bytes 98304 | tf_op jit(solution)/shard_map/concatenate | solution.py:541
  1.4 0.0 collective-permute-start.2
  1.4 1.5 %collective-permute-start = (bf16[192,128]{1,0:T(8,128)(2,1)S(1)}, bf16[192,128]{1,0:T(8,128)(2,1)S(1)}, u32[]{:S(2)}, u32[]{:S(2)}) collective-permute-start(bf16[192,128]{1,0:T(8,128)(2,1)S(1)} %pad_maximum_fusion.2.own), channel_id=1, source_target_pairs={{0,2},{2,0},{4,6},{6,4},{8,10},{10,8},{12,14},{14,12},{16,18},{18,... | collective-permute-start | bytes 147464 | tf_op jit(solution)/shard_map/ppermute | solution.py:506
  3.0 3.3 %collective-permute-start.1 = (bf16[192,128]{1,0:T(8,128)(2,1)S(1)}, bf16[192,128]{1,0:T(8,128)(2,1)S(1)}, u32[]{:S(2)}, u32[]{:S(2)}) collective-permute-start(bf16[192,128]{1,0:T(8,128)(2,1)S(1)} %pad_maximum_fusion.2.own), channel_id=1, source_target_pairs={{2,4},{4,2},{6,8},{8,6},{10,12},{12,10},{14,16},{16,14},{18,20},{2... | collective-permute-start | bytes 147464 | tf_op jit(solution)/shard_map/ppermute | solution.py:506
  6.2 0.0 copy-done.2
  6.2 0.1 collective-permute-start.3
  6.3 0.1 pad_add_fusion.place
  6.4 0.0 collective-permute-done.2
  6.4 2.6 %shard_map.113 = (bf16[784,256]{1,0:T(8,128)(2,1)S(1)}, bf16[192,240]{1,0:T(8,128)(2,1)S(1)}, s32[8,128]{1,0:T(8,128)S(1)}) custom-call(s32[4]{0:T(128)S(1)} %pad_add_fusion.place, bf16[192,128]{1,0:T(8,128)(2,1)S(1)} %pad_maximum_fusion.2.own, bf16[1,192,128]{2,1,0:T(8,128)(2,1)S(1)} %bitcast.21, s32[1,128]{1,0:T(1,128)} %limit.1, s32[3,1,128]{2,1,0:T(1,128)} %indices.1, ...), custom_call_target="tpu_custom_call" | custom-call | flops 2000000000 | bytes 4194304 | tf_op jit(solution)/shard_map/pallas_call | solution.py:544
  9.1 0.0 collective-permute-done.3
  9.1 0.0 collective-permute-done.odd_own
  9.1 1.6 %collective-permute-done.1.even_own = bf16[192,128]{1,0:T(8,128)(2,1)S(1)} collective-permute-done((bf16[192,128]{1,0:T(8,128)(2,1)S(1)}, bf16[192,128]{1,0:T(8,128)(2,1)S(1)}, u32[]{:S(2)}, u32[]{:S(2)}) %collective-permute-start.1) | collective-permute-done | bytes 49184 | tf_op jit(solution)/shard_map/ppermute | solution.py:506
  10.7 0.0 collective-permute-start.4
  10.7 0.5 %collective-permute-start.5 = (bf16[192,128]{1,0:T(8,128)(2,1)S(1)}, bf16[192,128]{1,0:T(8,128)(2,1)S(1)}, u32[]{:S(2)}, u32[]{:S(2)}) collective-permute-start(bf16[192,128]{1,0:T(8,128)(2,1)S(1)} %collective-permute-done.1.even_own), channel_id=1, source_target_pairs={{0,1},{1,0},{2,3},{3,2},{4,5},{5,4},{6,7},{7,6},{8,9},{9,8},{10,11... | collective-permute-start | bytes 147464 | tf_op jit(solution)/shard_map/ppermute | solution.py:486
  11.2 0.0 collective-permute-start.6
  11.2 1.2 %collective-permute-done.6 = s32[8,128]{1,0:T(8,128)S(1)} collective-permute-done((s32[8,128]{1,0:T(8,128)S(1)}, s32[8,128]{1,0:T(8,128)S(1)}, u32[]{:S(2)}, u32[]{:S(2)}) %collective-permute-start.6) | collective-permute-done | bytes 4128 | tf_op jit(solution)/shard_map/ppermute | solution.py:486
  12.4 0.0 collective-permute-done.4
  12.4 0.0 collective-permute-done.5
  12.4 0.0 copy-start.1
  12.4 0.0 slice-start
  12.4 4.1 %shard_map.114 = (bf16[64,128]{1,0:T(8,128)(2,1)S(1)}, bf16[64,128]{1,0:T(8,128)(2,1)S(1)}, bf16[64,128]{1,0:T(8,128)(2,1)S(1)}, bf16[64,128]{1,0:T(8,128)(2,1)S(1)}) custom-call(s32[4]{0:T(128)S(1)} %pad_add_fusion.place, f32[8]{0:T(128)} %gain.1, bf16[192,128]{1,0:T(8,128)(2,1)S(1)} %collective-permute-done.odd_own, bf16[1,192,128]{2,1,0:T(8,128)(2,1)S(1)} %bitcast.22, ...), custom_call_target="tpu_custom_call" | custom-call | flops 5000000000 | bytes 16777216 | tf_op jit(solution)/shard_map/pallas_call | solution.py:579
  16.5 0.0 copy-start
  16.5 1.6 %collective-permute-start.7 = (bf16[64,128]{1,0:T(8,128)(2,1)S(1)}, bf16[64,128]{1,0:T(8,128)(2,1)S(1)}, u32[]{:S(2)}, u32[]{:S(2)}) collective-permute-start(bf16[64,128]{1,0:T(8,128)(2,1)S(1)} %get-tuple-element.29), channel_id=1, source_target_pairs={{0,6},{2,4},{4,2},{6,0},{8,14},{10,12},{12,10},{14,8},{16,22},{18,... | collective-permute-start | bytes 49160 | tf_op jit(solution)/shard_map/ppermute | solution.py:506
  18.1 0.6 %collective-permute-start.8 = (bf16[64,128]{1,0:T(8,128)(2,1)S(1)}, bf16[64,128]{1,0:T(8,128)(2,1)S(1)}, u32[]{:S(2)}, u32[]{:S(2)}) collective-permute-start(bf16[64,128]{1,0:T(8,128)(2,1)S(1)} %get-tuple-element.30), channel_id=1, source_target_pairs={{0,2},{2,0},{4,6},{6,4},{8,10},{10,8},{12,14},{14,12},{16,18},{18,... | collective-permute-start | bytes 49160 | tf_op jit(solution)/shard_map/ppermute | solution.py:506
  18.7 1.4 %collective-permute-start.9 = (bf16[64,128]{1,0:T(8,128)(2,1)S(1)}, bf16[64,128]{1,0:T(8,128)(2,1)S(1)}, u32[]{:S(2)}, u32[]{:S(2)}) collective-permute-start(bf16[64,128]{1,0:T(8,128)(2,1)S(1)} %get-tuple-element.31), channel_id=1, source_target_pairs={{0,4},{2,6},{4,0},{6,2},{8,12},{10,14},{12,8},{14,10},{16,20},{18,... | collective-permute-start | bytes 49160 | tf_op jit(solution)/shard_map/ppermute | solution.py:506
  20.1 0.0 copy-done.1
  20.1 0.0 slice-done
  20.1 0.1 pad_maximum_fusion
  20.3 0.9 %collective-permute-done.7 = bf16[64,128]{1,0:T(8,128)(2,1)S(1)} collective-permute-done((bf16[64,128]{1,0:T(8,128)(2,1)S(1)}, bf16[64,128]{1,0:T(8,128)(2,1)S(1)}, u32[]{:S(2)}, u32[]{:S(2)}) %collective-permute-start.7) | collective-permute-done | bytes 16416 | tf_op jit(solution)/shard_map/ppermute | solution.py:506
  21.2 0.6 %collective-permute-done.8 = bf16[64,128]{1,0:T(8,128)(2,1)S(1)} collective-permute-done((bf16[64,128]{1,0:T(8,128)(2,1)S(1)}, bf16[64,128]{1,0:T(8,128)(2,1)S(1)}, u32[]{:S(2)}, u32[]{:S(2)}) %collective-permute-start.8) | collective-permute-done | bytes 16416 | tf_op jit(solution)/shard_map/ppermute | solution.py:506
  21.8 0.6 %collective-permute-done.9 = bf16[64,128]{1,0:T(8,128)(2,1)S(1)} collective-permute-done((bf16[64,128]{1,0:T(8,128)(2,1)S(1)}, bf16[64,128]{1,0:T(8,128)(2,1)S(1)}, u32[]{:S(2)}, u32[]{:S(2)}) %collective-permute-start.9) | collective-permute-done | bytes 16416 | tf_op jit(solution)/shard_map/ppermute | solution.py:506
  22.4 2.7 %collective-permute-start.10 = (bf16[4,64,128]{2,1,0:T(8,128)(2,1)S(1)}, bf16[4,64,128]{2,1,0:T(8,128)(2,1)S(1)}, u32[]{:S(2)}, u32[]{:S(2)}) collective-permute-start(bf16[4,64,128]{2,1,0:T(8,128)(2,1)S(1)} %pad_maximum_fusion.1.own), channel_id=1, source_target_pairs={{0,16},{2,18},{4,20},{6,22},{8,24},{10,26},{12,28},{14,30},{16,0},... | collective-permute-start | bytes 196616 | tf_op jit(solution)/shard_map/ppermute | solution.py:506
  25.1 0.4 collective-permute-start.11
  25.5 2.3 %collective-permute-start.12 = (bf16[4,64,128]{2,1,0:T(8,128)(2,1)S(1)}, bf16[4,64,128]{2,1,0:T(8,128)(2,1)S(1)}, u32[]{:S(2)}, u32[]{:S(2)}) collective-permute-start(bf16[4,64,128]{2,1,0:T(8,128)(2,1)S(1)} %pad_maximum_fusion.1.own), channel_id=1, source_target_pairs={{8,16},{10,18},{12,20},{14,22},{16,8},{18,10},{20,12},{22,14},{9,1... | collective-permute-start | bytes 196616 | tf_op jit(solution)/shard_map/ppermute | solution.py:506
  27.9 0.3 collective-permute-done.10.far_c.far_d
  28.2 1.2 %collective-permute-done.11.near_a = bf16[4,64,128]{2,1,0:T(8,128)(2,1)S(1)} collective-permute-done((bf16[4,64,128]{2,1,0:T(8,128)(2,1)S(1)}, bf16[4,64,128]{2,1,0:T(8,128)(2,1)S(1)}, u32[]{:S(2)}, u32[]{:S(2)}) %collective-permute-start.11) | collective-permute-done | bytes 65568 | tf_op jit(solution)/shard_map/ppermute | solution.py:506
  29.4 2.3 %collective-permute-done.12.near_b = bf16[4,64,128]{2,1,0:T(8,128)(2,1)S(1)} collective-permute-done((bf16[4,64,128]{2,1,0:T(8,128)(2,1)S(1)}, bf16[4,64,128]{2,1,0:T(8,128)(2,1)S(1)}, u32[]{:S(2)}, u32[]{:S(2)}) %collective-permute-start.12) | collective-permute-done | bytes 65568 | tf_op jit(solution)/shard_map/ppermute | solution.py:506
  31.7 0.0 copy-done
  31.7 6.5 %shard_map.115 = (bf16[64,128]{1,0:T(8,128)(2,1)S(1)}, bf16[64,128]{1,0:T(8,128)(2,1)S(1)}, bf16[64,128]{1,0:T(8,128)(2,1)S(1)}, bf16[64,128]{1,0:T(8,128)(2,1)S(1)}) custom-call(s32[4]{0:T(128)S(1)} %pad_add_fusion.place, bf16[4,64,128]{2,1,0:T(8,128)(2,1)S(1)} %pad_maximum_fusion.1.own, bf16[4,64,128]{2,1,0:T(8,128)(2,1)S(1)} %collective-permute-done.10.far_c.far_d, ...), custom_call_target="tpu_custom_call" | custom-call | tf_op jit(solution)/shard_map/pallas_call | solution.py:614
  38.2 1.1 %collective-permute-start.13 = (bf16[64,128]{1,0:T(8,128)(2,1)S(1)}, bf16[64,128]{1,0:T(8,128)(2,1)S(1)}, u32[]{:S(2)}, u32[]{:S(2)}) collective-permute-start(bf16[64,128]{1,0:T(8,128)(2,1)S(1)} %get-tuple-element.35), channel_id=1, source_target_pairs={{0,6},{2,4},{4,2},{6,0},{8,14},{10,12},{12,10},{14,8},{16,22},{18,... | collective-permute-start | bytes 49160 | tf_op jit(solution)/shard_map/ppermute | solution.py:506
  39.3 1.8 %collective-permute-start.14 = (bf16[64,128]{1,0:T(8,128)(2,1)S(1)}, bf16[64,128]{1,0:T(8,128)(2,1)S(1)}, u32[]{:S(2)}, u32[]{:S(2)}) collective-permute-start(bf16[64,128]{1,0:T(8,128)(2,1)S(1)} %get-tuple-element.36), channel_id=1, source_target_pairs={{0,2},{2,0},{4,6},{6,4},{8,10},{10,8},{12,14},{14,12},{16,18},{18,... | collective-permute-start | bytes 49160 | tf_op jit(solution)/shard_map/ppermute | solution.py:506
  41.1 0.6 %collective-permute-start.15 = (bf16[64,128]{1,0:T(8,128)(2,1)S(1)}, bf16[64,128]{1,0:T(8,128)(2,1)S(1)}, u32[]{:S(2)}, u32[]{:S(2)}) collective-permute-start(bf16[64,128]{1,0:T(8,128)(2,1)S(1)} %get-tuple-element.37), channel_id=1, source_target_pairs={{0,4},{2,6},{4,0},{6,2},{8,12},{10,14},{12,8},{14,10},{16,20},{18,... | collective-permute-start | bytes 49160 | tf_op jit(solution)/shard_map/ppermute | solution.py:506
  41.7 1.1 %collective-permute-done.13.from_1 = bf16[64,128]{1,0:T(8,128)(2,1)S(1)} collective-permute-done((bf16[64,128]{1,0:T(8,128)(2,1)S(1)}, bf16[64,128]{1,0:T(8,128)(2,1)S(1)}, u32[]{:S(2)}, u32[]{:S(2)}) %collective-permute-start.13) | collective-permute-done | bytes 16416 | tf_op jit(solution)/shard_map/ppermute | solution.py:506
  42.9 0.1 collective-permute-done.14.from_2
  43.0 1.8 %collective-permute-done.15.from_3 = bf16[64,128]{1,0:T(8,128)(2,1)S(1)} collective-permute-done((bf16[64,128]{1,0:T(8,128)(2,1)S(1)}, bf16[64,128]{1,0:T(8,128)(2,1)S(1)}, u32[]{:S(2)}, u32[]{:S(2)}) %collective-permute-start.15) | collective-permute-done | bytes 16416 | tf_op jit(solution)/shard_map/ppermute | solution.py:506
  44.9 1.2 %shard_map.116 = (f32[1,128]{1,0:T(1,128)}, bf16[1,128,128]{2,1,0:T(8,128)(2,1)}) custom-call(s32[4]{0:T(128)S(1)} %pad_add_fusion.place, bf16[64,128]{1,0:T(8,128)(2,1)S(1)} %get-tuple-element.34.from_0, bf16[64,128]{1,0:T(8,128)(2,1)S(1)} %collective-permute-done.13.from_1, bf16[64,128]{1,0:T(8,128)(2,1)S(1)} %collective-permute-done.14.from_2, ...), custom_call_target="tpu_custom_call" | custom-call | tf_op jit(solution)/shard_map/pallas_call | solution.py:638
  (3 shorter events, 0.1 us)
Async XLA Ops:
  0.6 5.6 %copy-start.2 = (bf16[1,128,128]{2,1,0:T(8,128)(2,1)S(1)}, bf16[1,128,128]{2,1,0:T(8,128)(2,1)}, u32[]{:S(2)}) copy-start(bf16[1,128,128]{2,1,0:T(8,128)(2,1)} %param.14) | copy-start | bytes 98308
  1.4 5.0 %collective-permute-start.2 = (bf16[192,128]{1,0:T(8,128)(2,1)S(1)}, bf16[192,128]{1,0:T(8,128)(2,1)S(1)}, u32[]{:S(2)}, u32[]{:S(2)}) collective-permute-start(bf16[192,128]{1,0:T(8,128)(2,1)S(1)} %pad_maximum_fusion.2.own), channel_id=1, source_target_pairs={{0,1},{1,0},{2,3},{3,2},{4,5},{5,4},{6,7},{7,6},{8,9},{9,8},{10,11... | collective-permute-start | bytes 147464 | tf_op jit(solution)/shard_map/ppermute | solution.py:486
  1.4 7.7 %collective-permute-start = (bf16[192,128]{1,0:T(8,128)(2,1)S(1)}, bf16[192,128]{1,0:T(8,128)(2,1)S(1)}, u32[]{:S(2)}, u32[]{:S(2)}) collective-permute-start(bf16[192,128]{1,0:T(8,128)(2,1)S(1)} %pad_maximum_fusion.2.own), channel_id=1, source_target_pairs={{0,2},{2,0},{4,6},{6,4},{8,10},{10,8},{12,14},{14,12},{16,18},{18,... | collective-permute-start | bytes 147464 | tf_op jit(solution)/shard_map/ppermute | solution.py:506
  3.0 7.8 %collective-permute-start.1 = (bf16[192,128]{1,0:T(8,128)(2,1)S(1)}, bf16[192,128]{1,0:T(8,128)(2,1)S(1)}, u32[]{:S(2)}, u32[]{:S(2)}) collective-permute-start(bf16[192,128]{1,0:T(8,128)(2,1)S(1)} %pad_maximum_fusion.2.own), channel_id=1, source_target_pairs={{2,4},{4,2},{6,8},{8,6},{10,12},{12,10},{14,16},{16,14},{18,20},{2... | collective-permute-start | bytes 147464 | tf_op jit(solution)/shard_map/ppermute | solution.py:506
  6.2 2.8 %collective-permute-start.3 = (bf16[128,128]{1,0:T(8,128)(2,1)S(1)}, bf16[128,128]{1,0:T(8,128)(2,1)S(1)}, u32[]{:S(2)}, u32[]{:S(2)}) collective-permute-start(bf16[128,128]{1,0:T(8,128)(2,1)S(1)} %bitcast.34), channel_id=1, source_target_pairs={{0,1},{1,0},{2,3},{3,2},{4,5},{5,4},{6,7},{7,6},{8,9},{9,8},{10,11... | collective-permute-start | bytes 98312 | tf_op jit(solution)/shard_map/ppermute | solution.py:486
  10.7 1.7 %collective-permute-start.4 = (bf16[192,128]{1,0:T(8,128)(2,1)S(1)}, bf16[192,128]{1,0:T(8,128)(2,1)S(1)}, u32[]{:S(2)}, u32[]{:S(2)}) collective-permute-start(bf16[192,128]{1,0:T(8,128)(2,1)S(1)} %collective-permute-done.odd_own), channel_id=1, source_target_pairs={{0,1},{1,0},{2,3},{3,2},{4,5},{5,4},{6,7},{7,6},{8,9},{9,8},{10,11... | collective-permute-start | bytes 147464 | tf_op jit(solution)/shard_map/ppermute | solution.py:486
  10.7 1.7 %collective-permute-start.5 = (bf16[192,128]{1,0:T(8,128)(2,1)S(1)}, bf16[192,128]{1,0:T(8,128)(2,1)S(1)}, u32[]{:S(2)}, u32[]{:S(2)}) collective-permute-start(bf16[192,128]{1,0:T(8,128)(2,1)S(1)} %collective-permute-done.1.even_own), channel_id=1, source_target_pairs={{0,1},{1,0},{2,3},{3,2},{4,5},{5,4},{6,7},{7,6},{8,9},{9,8},{10,11... | collective-permute-start | bytes 147464 | tf_op jit(solution)/shard_map/ppermute | solution.py:486
  11.2 1.2 %collective-permute-start.6 = (s32[8,128]{1,0:T(8,128)S(1)}, s32[8,128]{1,0:T(8,128)S(1)}, u32[]{:S(2)}, u32[]{:S(2)}) collective-permute-start(s32[8,128]{1,0:T(8,128)S(1)} %get-tuple-element.24.marks), channel_id=1, source_target_pairs={{0,1},{1,0},{2,3},{3,2},{4,5},{5,4},{6,7},{7,6},{8,9},{9,8},{10,11... | collective-permute-start | bytes 12296 | tf_op jit(solution)/shard_map/ppermute | solution.py:486
  12.4 7.7 %copy-start.1 = (bf16[3,3,9,384]{3,1,2,0:T(4,128)(2,1)S(1)}, bf16[3,3,9,384]{3,1,2,0:T(4,128)(2,1)}, u32[]{:S(2)}) copy-start(bf16[3,3,9,384]{3,1,2,0:T(4,128)(2,1)} %param.18) | copy-start | bytes 186628
  12.4 7.7 %slice-start = ((bf16[3,3,9,384]{3,1,2,0:T(4,128)(2,1)}), bf16[3,3,8,384]{3,1,2,0:T(4,128)(2,1)S(1)}, s32[]{:S(2)}) async-start(bf16[3,3,9,384]{3,1,2,0:T(4,128)(2,1)} %param.18), calls=%async_computation | async-start | bytes 147456 | tf_op jit(solution)/shard_map/slice | solution.py:574
  16.5 15.2 %copy-start = (bf16[3,3,128,384]{3,2,1,0:T(8,128)(2,1)S(1)}, bf16[3,3,128,384]{3,2,1,0:T(8,128)(2,1)}, u32[]{:S(2)}) copy-start(bf16[3,3,128,384]{3,2,1,0:T(8,128)(2,1)} %param.17) | copy-start | bytes 2654212
  16.5 4.7 %collective-permute-start.7 = (bf16[64,128]{1,0:T(8,128)(2,1)S(1)}, bf16[64,128]{1,0:T(8,128)(2,1)S(1)}, u32[]{:S(2)}, u32[]{:S(2)}) collective-permute-start(bf16[64,128]{1,0:T(8,128)(2,1)S(1)} %get-tuple-element.29), channel_id=1, source_target_pairs={{0,6},{2,4},{4,2},{6,0},{8,14},{10,12},{12,10},{14,8},{16,22},{18,... | collective-permute-start | bytes 49160 | tf_op jit(solution)/shard_map/ppermute | solution.py:506
  18.1 3.7 %collective-permute-start.8 = (bf16[64,128]{1,0:T(8,128)(2,1)S(1)}, bf16[64,128]{1,0:T(8,128)(2,1)S(1)}, u32[]{:S(2)}, u32[]{:S(2)}) collective-permute-start(bf16[64,128]{1,0:T(8,128)(2,1)S(1)} %get-tuple-element.30), channel_id=1, source_target_pairs={{0,2},{2,0},{4,6},{6,4},{8,10},{10,8},{12,14},{14,12},{16,18},{18,... | collective-permute-start | bytes 49160 | tf_op jit(solution)/shard_map/ppermute | solution.py:506
  18.7 3.7 %collective-permute-start.9 = (bf16[64,128]{1,0:T(8,128)(2,1)S(1)}, bf16[64,128]{1,0:T(8,128)(2,1)S(1)}, u32[]{:S(2)}, u32[]{:S(2)}) collective-permute-start(bf16[64,128]{1,0:T(8,128)(2,1)S(1)} %get-tuple-element.31), channel_id=1, source_target_pairs={{0,4},{2,6},{4,0},{6,2},{8,12},{10,14},{12,8},{14,10},{16,20},{18,... | collective-permute-start | bytes 49160 | tf_op jit(solution)/shard_map/ppermute | solution.py:506
  22.4 5.7 %collective-permute-start.10 = (bf16[4,64,128]{2,1,0:T(8,128)(2,1)S(1)}, bf16[4,64,128]{2,1,0:T(8,128)(2,1)S(1)}, u32[]{:S(2)}, u32[]{:S(2)}) collective-permute-start(bf16[4,64,128]{2,1,0:T(8,128)(2,1)S(1)} %pad_maximum_fusion.1.own), channel_id=1, source_target_pairs={{0,16},{2,18},{4,20},{6,22},{8,24},{10,26},{12,28},{14,30},{16,0},... | collective-permute-start | bytes 196616 | tf_op jit(solution)/shard_map/ppermute | solution.py:506
  25.1 4.3 %collective-permute-start.11 = (bf16[4,64,128]{2,1,0:T(8,128)(2,1)S(1)}, bf16[4,64,128]{2,1,0:T(8,128)(2,1)S(1)}, u32[]{:S(2)}, u32[]{:S(2)}) collective-permute-start(bf16[4,64,128]{2,1,0:T(8,128)(2,1)S(1)} %pad_maximum_fusion.1.own), channel_id=1, source_target_pairs={{0,8},{2,10},{4,12},{6,14},{8,0},{10,2},{12,4},{14,6},{16,24},{18,... | collective-permute-start | bytes 196616 | tf_op jit(solution)/shard_map/ppermute | solution.py:506
  25.5 6.1 %collective-permute-start.12 = (bf16[4,64,128]{2,1,0:T(8,128)(2,1)S(1)}, bf16[4,64,128]{2,1,0:T(8,128)(2,1)S(1)}, u32[]{:S(2)}, u32[]{:S(2)}) collective-permute-start(bf16[4,64,128]{2,1,0:T(8,128)(2,1)S(1)} %pad_maximum_fusion.1.own), channel_id=1, source_target_pairs={{8,16},{10,18},{12,20},{14,22},{16,8},{18,10},{20,12},{22,14},{9,1... | collective-permute-start | bytes 196616 | tf_op jit(solution)/shard_map/ppermute | solution.py:506
  38.2 4.7 %collective-permute-start.13 = (bf16[64,128]{1,0:T(8,128)(2,1)S(1)}, bf16[64,128]{1,0:T(8,128)(2,1)S(1)}, u32[]{:S(2)}, u32[]{:S(2)}) collective-permute-start(bf16[64,128]{1,0:T(8,128)(2,1)S(1)} %get-tuple-element.35), channel_id=1, source_target_pairs={{0,6},{2,4},{4,2},{6,0},{8,14},{10,12},{12,10},{14,8},{16,22},{18,... | collective-permute-start | bytes 49160 | tf_op jit(solution)/shard_map/ppermute | solution.py:506
  39.3 3.7 %collective-permute-start.14 = (bf16[64,128]{1,0:T(8,128)(2,1)S(1)}, bf16[64,128]{1,0:T(8,128)(2,1)S(1)}, u32[]{:S(2)}, u32[]{:S(2)}) collective-permute-start(bf16[64,128]{1,0:T(8,128)(2,1)S(1)} %get-tuple-element.36), channel_id=1, source_target_pairs={{0,2},{2,0},{4,6},{6,4},{8,10},{10,8},{12,14},{14,12},{16,18},{18,... | collective-permute-start | bytes 49160 | tf_op jit(solution)/shard_map/ppermute | solution.py:506
  41.1 3.7 %collective-permute-start.15 = (bf16[64,128]{1,0:T(8,128)(2,1)S(1)}, bf16[64,128]{1,0:T(8,128)(2,1)S(1)}, u32[]{:S(2)}, u32[]{:S(2)}) collective-permute-start(bf16[64,128]{1,0:T(8,128)(2,1)S(1)} %get-tuple-element.37), channel_id=1, source_target_pairs={{0,4},{2,6},{4,0},{6,2},{8,12},{10,14},{12,8},{14,10},{16,20},{18,... | collective-permute-start | bytes 49160 | tf_op jit(solution)/shard_map/ppermute | solution.py:506
where the time goes:
time: 46.4 us; the launch traced here: 46 us
  starting transfers between devices  18 us (39%)
  Pallas kernels  14.4 us (31%)
  waiting for transfers between devices  11.9 us (26%)
  other arithmetic  0.97 us (2%)
  between operations  0.77 us (2%)
    ppermute x11, starting transfers between devices, to_rows(): lax.ppermute(value, 'band', [(i, shift(i)) for i in range(bands) if 0 <=...  17.4 us
    ppermute x11, waiting for transfers between devices, to_rows(): lax.ppermute(value, 'band', [(i, shift(i)) for i in range(bands) if 0 <=...  10.7 us
    pallas_call x1, Pallas kernels, local(): pl.pallas_call(refine_kernel, out_shape=(jax.ShapeDtypeStruct((2 * STRIP,...  6.5 us
    pallas_call x1, Pallas kernels, local(): pl.pallas_call(volume_kernel, out_shape=(jax.ShapeDtypeStruct((BLOCK_ROWS...  4.08 us
    pallas_call x1, Pallas kernels, local(): pl.pallas_call(own_row_kernel, out_shape=(jax.ShapeDtypeStruct((padded, 2...  2.64 us
    pallas_call x1, Pallas kernels, local(): pl.pallas_call(unpack_kernel, out_shape=(jax.ShapeDtypeStruct((1, TILE),...  1.18 us
    ppermute x5, waiting for transfers between devices, to_sides(): return lax.ppermute(value, 'disp', right + left)[None]  1.17 us
  transfers between devices with their start and end apart: 16, of which 11 were waited for; matrix products, arithmetic and copies ran while one was open for 1% of the time, Pallas kernels for 6%

commit v1 on v0

--- a/solution.py
+++ b/solution.py
@@ -31,6 +31,13 @@
 
 f32 = jnp.float32
 bf16 = jnp.bfloat16
+
+
+def position():
+    return (
+        lax.axis_index("band"), lax.axis_index("disp"),
+        lax.axis_size("band"), lax.axis_size("disp"),
+    )
 
 
 def dot(a, b):
@@ -147,11 +154,21 @@
 
 
 def own_row_kernel(
-    place, own, across, limit, indices, vol_kernel, raw_out, taps_out, marks_out, wide, extra,
-    kernel, sem,
+    own, across, limit, indices, gain, head, vol_kernel, raw_out, taps_out, marks_out, gains_out,
+    heads_out, wide, extra, limits, index_rows, gain_held, head_held, kernel, sems,
 ):
-    copy = pltpu.make_async_copy(vol_kernel, kernel, sem.at[0])
-    copy.start()
+    place = position()
+    copies = [
+        pltpu.make_async_copy(source, target, sems.at[i])
+        for i, (source, target) in enumerate(
+            (
+                (limit, limits), (indices, index_rows), (gain, gain_held), (head, head_held),
+                (vol_kernel, kernel),
+            )
+        )
+    ]
+    for copy in copies:
+        copy.start()
     tiles = [across[0], own[...], across[across.shape[0] - 1]]
     tiles = [tile.astype(f32) for tile in tiles]
     correlate(
@@ -159,17 +176,26 @@
         place, 1.0, wide, extra,
     )
     raw_out[...] = jnp.concatenate([wide[...], extra[...]], axis=1).astype(bf16)
-    marks = [limit[...]] + [indices[t] for t in range(ITERS)]
+    for copy in copies:
+        copy.wait()
+    marks = [limits[...]] + [index_rows[t] for t in range(ITERS)]
     blank = jnp.zeros((GROUPS - len(marks), TILE), jnp.int32)
     marks_out[...] = jnp.concatenate(marks + [blank], axis=0)
-    copy.wait()
+    group_at = lax.broadcasted_iota(jnp.int32, (GROUPS, TILE), 0)
+    gains = jnp.zeros((GROUPS, TILE), f32)
+    for g in range(GROUPS):
+        gains = jnp.where(group_at == g, gain_held[g], gains)
+    gains_out[...] = gains
+    heads = head_held[...].astype(f32) * feature_scale
+    heads_out[...] = jnp.broadcast_to(heads, heads_out.shape).astype(bf16)
     taps_out[...] = toeplitz(kernel)
 
 
 def volume_kernel(
-    place, gain, odd_own, odd_across, even_own, even_across, marks, marks_across, hidden,
+    gains, odd_own, odd_across, even_own, even_across, marks, marks_across, hidden,
     hidden_across, raw_own, taps_own, out_0, out_1, out_2, out_3, raw, taps, wide, extra, logit, padded, blocks, sems,
 ):
+    place = position()
     band, bands = place[0], place[2]
     is_even = band % 2 == 0
     copies = [
@@ -201,9 +227,6 @@
     levels_of = [marks[...], jnp.where(lane < EDGE, marks_across[last], left_marks)]
     lane8 = lax.broadcasted_iota(jnp.int32, (OUT_SLAB, TILE), 1)
     group_at = lax.broadcasted_iota(jnp.int32, (GROUPS, TILE), 0)
-    gains = jnp.zeros((GROUPS, TILE), f32)
-    for g in range(GROUPS):
-        gains = jnp.where(group_at == g, gain[g], gains)
     wanted = [
         [jnp.broadcast_to(rows[t + 1 : t + 2], (GROUPS, TILE)) for t in range(ITERS)]
         for rows in levels_of
@@ -244,7 +267,7 @@
         for i in range(2):
             volume = centre[:, i * TILE : (i + 1) * TILE] + jnp.maximum(convs[i], 0.0)
             volume = volume.astype(bf16).astype(f32).reshape(BLOCK, GROUPS, TILE)
-            logit[i, q * BLOCK : (q + 1) * BLOCK, :] = jnp.sum(volume * gains[None], axis=1)
+            logit[i, q * BLOCK : (q + 1) * BLOCK, :] = jnp.sum(volume * gains[...][None], axis=1)
             for d in range(BLOCK):
                 for t in range(ITERS):
                     hit = wanted[i][t] == q * BLOCK + d
@@ -319,7 +342,6 @@
 
 
 def refine_kernel(
-    place,
     own,
     far_c,
     far_d,
@@ -327,7 +349,7 @@
     near_b,
     hid_weight,
     in_weight,
-    head,
+    heads,
     out_0,
     out_1,
     out_2,
@@ -356,7 +378,8 @@
     for copy in copies:
         copy.start()
 
-    band, disp, bands, disps = place[0], place[1], place[2], place[3]
+    place = position()
+    band, disp, bands, disps = place
     member, layer = band % QUAD, band // QUAD
     at = strip_at(place, member)
     first = strip * at - EDGE
@@ -408,7 +431,6 @@
     keep(line, taps, 0, hidden_at[...])
     for copy in copies:
         copy.wait()
-    heads = jnp.broadcast_to(head[...].astype(f32) * feature_scale, (HID_CH, HID_CH)).astype(bf16)
 
     for t in range(ITERS):
         low, high = 1 + 2 * t, rows - 2 - 2 * t
@@ -444,7 +466,7 @@
         inside = ((column >= 0) | (disp > 0)) & ((column < TILE) | (disp < disps - 1))
         inside = inside & (row >= 0) & (row < bands)
         hidden = jnp.where(inside, hidden, 0.0).astype(bf16)
-        level[EDGE + at : EDGE + at + length, :] += dot_nt(hidden, heads)
+        level[EDGE + at : EDGE + at + length, :] += dot_nt(hidden, heads[...])
         hidden_at[at : at + length, :] = hidden.astype(f32)
         if t < ITERS - 1:
             keep(line, taps, at, hidden.astype(f32))
@@ -463,9 +485,10 @@
         out[...] = blocks[member ^ i]
 
 
-def unpack_kernel(place, from_0, from_1, from_2, from_3, disparity_out, hidden_out, blocks):
+def unpack_kernel(from_0, from_1, from_2, from_3, disparity_out, hidden_out, blocks):
     for i, block in enumerate((from_0, from_1, from_2, from_3)):
         blocks[i] = block[...]
+    place = position()
     member = place[0] % QUAD
     slots = [slot_of(strip_at(place, strip) ^ member) for strip in range(QUAD)]
     held = [blocks[slot].astype(f32) for slot in slots]
@@ -529,10 +552,6 @@
     head_weight,
 ):
     bands, disps = lax.axis_size("band"), lax.axis_size("disp")
-    place = jnp.stack(
-        [lax.axis_index("band"), lax.axis_index("disp"), jnp.int32(bands), jnp.int32(disps)]
-    ).astype(jnp.int32)
-    smem = pl.BlockSpec(memory_space=pltpu.SMEM)
     vmem = pl.BlockSpec(memory_space=pltpu.VMEM)
     hbm = pl.BlockSpec(memory_space=pltpu.HBM)
     anywhere = pl.BlockSpec(memory_space=pl.ANY)
@@ -541,26 +560,32 @@
     feats = jnp.concatenate([feat_left[0], feat_right[0]], axis=0)
     odd_own, even_own = to_rows(feats, odd_pair), to_rows(feats, even_pair)
     across = to_sides(feats)
-    raw_own, taps, marks = pl.pallas_call(
+    raw_own, taps, marks, gains, heads = pl.pallas_call(
         own_row_kernel,
         out_shape=(
             jax.ShapeDtypeStruct((padded, 2 * TILE), bf16),
             jax.ShapeDtypeStruct((3 * OUT_SLAB, 3 * SLAB), bf16),
             jax.ShapeDtypeStruct((GROUPS, TILE), jnp.int32),
+            jax.ShapeDtypeStruct((GROUPS, TILE), f32),
+            jax.ShapeDtypeStruct((HID_CH, HID_CH), bf16),
         ),
-        in_specs=[smem, vmem, vmem, vmem, vmem, hbm],
-        out_specs=(vmem, vmem, vmem),
+        in_specs=[vmem, vmem] + [hbm] * 5,
+        out_specs=(vmem,) * 5,
         scratch_shapes=[
             pltpu.VMEM((padded, TILE), f32),
             pltpu.VMEM((padded, TILE), f32),
+            pltpu.VMEM((1, TILE), jnp.int32),
+            pltpu.VMEM((ITERS, 1, TILE), jnp.int32),
+            pltpu.SMEM((GROUPS,), f32),
+            pltpu.VMEM((1, HID_CH), bf16),
             pltpu.VMEM((27, GROUPS, GROUPS), bf16),
-            pltpu.SemaphoreType.DMA((1,)),
+            pltpu.SemaphoreType.DMA((5,)),
         ],
         compiler_params=pltpu.CompilerParams(vmem_limit_bytes=16 * 2**20),
         cost_estimate=pl.CostEstimate(flops=2 * 10**9, bytes_accessed=4 * 2**20, transcendentals=0),
     )(
-        place, feats, across, in_hbm(limit), in_hbm(indices),
-        in_hbm(vol_kernel.reshape(27, GROUPS, GROUPS)),
+        feats, across, in_hbm(limit), in_hbm(indices), in_hbm(group_gain),
+        in_hbm(head_weight.reshape(1, HID_CH)), in_hbm(vol_kernel.reshape(27, GROUPS, GROUPS)),
     )
     hidden = hidden_start[0]
     hidden_across = to_sides(hidden)
@@ -579,7 +604,7 @@
     blocks = pl.pallas_call(
         volume_kernel,
         out_shape=(jax.ShapeDtypeStruct((BLOCK_ROWS, TILE), bf16),) * QUAD,
-        in_specs=[smem, smem] + [vmem] * 8 + [hbm, hbm],
+        in_specs=[vmem] * 9 + [hbm, hbm],
         out_specs=(vmem,) * QUAD,
         scratch_shapes=[
             pltpu.VMEM((padded, 2 * TILE), bf16),
@@ -596,8 +621,8 @@
             flops=5 * 10**9, bytes_accessed=16 * 2**20, transcendentals=DISPS * TILE
         ),
     )(
-        place, in_hbm(group_gain), odd_own, odd_across, even_own, even_across,
-        marks, marks_across, in_hbm(hidden), hidden_across, raw_own, taps,
+        gains, odd_own, odd_across, even_own, even_across,
+        marks, marks_across, hidden, hidden_across, raw_own, taps,
     )
 
     own, in_weight = lax.optimization_barrier((jnp.stack(in_group(blocks)), in_weight))
@@ -614,7 +639,7 @@
     refined = pl.pallas_call(
         refine_kernel,
         out_shape=(jax.ShapeDtypeStruct((2 * STRIP, HID_CH), bf16),) * QUAD,
-        in_specs=[smem] + [vmem] * 5 + [anywhere, anywhere, vmem],
+        in_specs=[vmem] * 5 + [anywhere, anywhere, vmem],
         out_specs=(vmem,) * QUAD,
         scratch_shapes=[
             pltpu.VMEM((pixels + 2 * EDGE, HID_CH), f32),
@@ -631,9 +656,8 @@
         ],
         compiler_params=pltpu.CompilerParams(vmem_limit_bytes=32 * 2**20),
     )(
-        place, own, *around,
-        hid_kernel.reshape(9 * HID_CH, 3 * HID_CH), in_weight,
-        in_hbm(head_weight.reshape(1, HID_CH)),
+        own, *around,
+        hid_kernel.reshape(9 * HID_CH, 3 * HID_CH), in_weight, heads,
     )
     disparity, hidden = pl.pallas_call(
         unpack_kernel,
@@ -641,11 +665,11 @@
             jax.ShapeDtypeStruct((1, TILE), f32),
             jax.ShapeDtypeStruct((1, TILE, HID_CH), bf16),
         ),
-        in_specs=[smem] + [vmem] * QUAD,
+        in_specs=[vmem] * QUAD,
         out_specs=(vmem, vmem),
         scratch_shapes=[pltpu.VMEM((QUAD, 2 * STRIP, HID_CH), bf16)],
         compiler_params=pltpu.CompilerParams(vmem_limit_bytes=4 * 2**20),
-    )(place, *in_group(refined))
+    )(*in_group(refined))
     return (disparity, hidden)
 
 

time: 46.4 us -> 44.3 us (0.955)
  Pallas kernels: 14.4 us -> 11.7 us
  waiting for transfers between devices: 11.9 us -> 12.6 us
    pallas_call x1, Pallas kernels: 4.08 us -> 3.29 us  [local(): pl.pallas_call(volume_kernel, out_shape=(jax.ShapeDtypeStruct((BLOCK_ROWS...]
    ppermute x11, waiting for transfers between devices: 10.7 us -> 11.5 us  [to_rows(): lax.ppermute(value, 'band', [(i, shift(i)) for i in range(bands) if 0 <=...]
    pallas_call x1, Pallas kernels: 2.64 us -> 1.93 us  [local(): pl.pallas_call(own_row_kernel, out_shape=(jax.ShapeDtypeStruct((padded, 2...]
    pallas_call x1, Pallas kernels: 6.5 us -> 5.83 us  [local(): pl.pallas_call(refine_kernel, out_shape=(jax.ShapeDtypeStruct((2 * STRIP,...]
    pallas_call x1, Pallas kernels: 1.18 us -> 0.63 us  [local(): pl.pallas_call(unpack_kernel, out_shape=(jax.ShapeDtypeStruct((1, TILE),...]
  transfers between devices with their start and end apart: 16 -> 16, of which waited for: 11 -> 11; matrix products, arithmetic and copies ran while one was open for 1% -> 0% of each run, Pallas kernels for 6% -> 4%
where the time goes in v1:
time: 44.3 us; the launch traced here: 44 us
  starting transfers between devices  18 us (41%)
  waiting for transfers between devices  12.6 us (28%)
  Pallas kernels  11.7 us (26%)
  other arithmetic  0.9 us (2%)
  between operations  0.77 us (2%)
    ppermute x11, starting transfers between devices, to_rows(): lax.ppermute(value, 'band', [(i, shift(i)) for i in range(bands) if 0 <=...  17.4 us
    ppermute x11, waiting for transfers between devices, to_rows(): lax.ppermute(value, 'band', [(i, shift(i)) for i in range(bands) if 0 <=...  11.5 us
    pallas_call x1, Pallas kernels, local(): pl.pallas_call(refine_kernel, out_shape=(jax.ShapeDtypeStruct((2 * STRIP,...  5.83 us
    pallas_call x1, Pallas kernels, local(): pl.pallas_call(volume_kernel, out_shape=(jax.ShapeDtypeStruct((BLOCK_ROWS...  3.29 us
    pallas_call x1, Pallas kernels, local(): pl.pallas_call(own_row_kernel, out_shape=(jax.ShapeDtypeStruct((padded, 2...  1.93 us
    ppermute x5, waiting for transfers between devices, to_sides(): return lax.ppermute(value, 'disp', right + left)[None]  1.17 us
  transfers between devices with their start and end apart: 16, of which 11 were waited for; matrix products, arithmetic and copies ran while one was open for 0% of the time, Pallas kernels for 4%

profile of v1, /device:TPU:8, one launch (start us, length us, event | category | flops | bytes accessed | tf_op | source)
XLA Modules:
  0.0 44.0 jit_solution(1809392043260560610)
XLA Ops:
  0.6 0.0 copy-start.1
  0.6 0.8 %pad_maximum_fusion.2.own = bf16[192,128]{1,0:T(8,128)(2,1)S(1)} fusion(bf16[96,128]{1,0:T(8,128)(2,1)} %bitcast.26, bf16[96,128]{1,0:T(8,128)(2,1)} %bitcast.27), kind=kLoop, calls=%fused_computation.2 | loop fusion | flops 98304 | bytes 98304 | tf_op jit(solution)/shard_map/concatenate | solution.py:560
  1.4 0.0 collective-permute-start
  1.4 1.5 %collective-permute-start.1 = (bf16[192,128]{1,0:T(8,128)(2,1)S(1)}, bf16[192,128]{1,0:T(8,128)(2,1)S(1)}, u32[]{:S(2)}, u32[]{:S(2)}) collective-permute-start(bf16[192,128]{1,0:T(8,128)(2,1)S(1)} %pad_maximum_fusion.2.own), channel_id=1, source_target_pairs={{0,2},{2,0},{4,6},{6,4},{8,10},{10,8},{12,14},{14,12},{16,18},{18,... | collective-permute-start | bytes 147464 | tf_op jit(solution)/shard_map/ppermute | solution.py:529
  3.0 3.3 %collective-permute-start.2 = (bf16[192,128]{1,0:T(8,128)(2,1)S(1)}, bf16[192,128]{1,0:T(8,128)(2,1)S(1)}, u32[]{:S(2)}, u32[]{:S(2)}) collective-permute-start(bf16[192,128]{1,0:T(8,128)(2,1)S(1)} %pad_maximum_fusion.2.own), channel_id=1, source_target_pairs={{2,4},{4,2},{6,8},{8,6},{10,12},{12,10},{14,16},{16,14},{18,20},{2... | collective-permute-start | bytes 147464 | tf_op jit(solution)/shard_map/ppermute | solution.py:529
  6.2 0.0 copy-done.1
  6.2 0.1 collective-permute-start.3
  6.3 0.0 collective-permute-done
  6.3 1.9 %shard_map.113 = (bf16[784,256]{1,0:T(8,128)(2,1)S(1)}, bf16[192,240]{1,0:T(8,128)(2,1)S(1)}, s32[8,128]{1,0:T(8,128)S(1)}, f32[8,128]{1,0:T(8,128)S(1)}, bf16[128,128]{1,0:T(8,128)(2,1)S(1)}) custom-call(bf16[192,128]{1,0:T(8,128)(2,1)S(1)} %pad_maximum_fusion.2.own, bf16[1,192,128]{2,1,0:T(8,128)(2,1)S(1)} %bitcast.21, s32[1,128]{1,0:T(1,128)} %limit.1, ...), custom_call_target="tpu_custom_call" | custom-call | flops 2000000000 | bytes 4194304 | tf_op jit(solution)/shard_map/pallas_call | solution.py:563
  8.3 0.0 collective-permute-done.3
  8.3 0.0 collective-permute-done.1.odd_own
  8.3 2.4 %collective-permute-done.2.even_own = bf16[192,128]{1,0:T(8,128)(2,1)S(1)} collective-permute-done((bf16[192,128]{1,0:T(8,128)(2,1)S(1)}, bf16[192,128]{1,0:T(8,128)(2,1)S(1)}, u32[]{:S(2)}, u32[]{:S(2)}) %collective-permute-start.2) | collective-permute-done | bytes 49184 | tf_op jit(solution)/shard_map/ppermute | solution.py:529
  10.7 0.0 collective-permute-start.4
  10.7 0.5 %collective-permute-start.5 = (bf16[192,128]{1,0:T(8,128)(2,1)S(1)}, bf16[192,128]{1,0:T(8,128)(2,1)S(1)}, u32[]{:S(2)}, u32[]{:S(2)}) collective-permute-start(bf16[192,128]{1,0:T(8,128)(2,1)S(1)} %collective-permute-done.2.even_own), channel_id=1, source_target_pairs={{0,1},{1,0},{2,3},{3,2},{4,5},{5,4},{6,7},{7,6},{8,9},{9,8},{10,11... | collective-permute-start | bytes 147464 | tf_op jit(solution)/shard_map/ppermute | solution.py:509
  11.2 0.0 collective-permute-start.6
  11.2 1.2 %collective-permute-done.6 = s32[8,128]{1,0:T(8,128)S(1)} collective-permute-done((s32[8,128]{1,0:T(8,128)S(1)}, s32[8,128]{1,0:T(8,128)S(1)}, u32[]{:S(2)}, u32[]{:S(2)}) %collective-permute-start.6) | collective-permute-done | bytes 4128 | tf_op jit(solution)/shard_map/ppermute | solution.py:509
  12.4 0.0 collective-permute-done.4
  12.4 0.0 collective-permute-done.5
  12.4 0.0 copy-start.2
  12.4 0.0 slice-start
  12.4 3.3 %shard_map.114 = (bf16[64,128]{1,0:T(8,128)(2,1)S(1)}, bf16[64,128]{1,0:T(8,128)(2,1)S(1)}, bf16[64,128]{1,0:T(8,128)(2,1)S(1)}, bf16[64,128]{1,0:T(8,128)(2,1)S(1)}) custom-call(f32[8,128]{1,0:T(8,128)S(1)} %get-tuple-element.22.gains, bf16[192,128]{1,0:T(8,128)(2,1)S(1)} %collective-permute-done.1.odd_own, bf16[1,192,128]{2,1,0:T(8,128)(2,1)S(1)} %bitcast.19, ...), custom_call_target="tpu_custom_call" | custom-call | flops 5000000000 | bytes 16777216 | tf_op jit(solution)/shard_map/pallas_call | solution.py:604
  15.7 0.0 copy-start
  15.7 1.6 %collective-permute-start.7 = (bf16[64,128]{1,0:T(8,128)(2,1)S(1)}, bf16[64,128]{1,0:T(8,128)(2,1)S(1)}, u32[]{:S(2)}, u32[]{:S(2)}) collective-permute-start(bf16[64,128]{1,0:T(8,128)(2,1)S(1)} %get-tuple-element.32), channel_id=1, source_target_pairs={{0,6},{2,4},{4,2},{6,0},{8,14},{10,12},{12,10},{14,8},{16,22},{18,... | collective-permute-start | bytes 49160 | tf_op jit(solution)/shard_map/ppermute | solution.py:529
  17.3 0.6 %collective-permute-start.8 = (bf16[64,128]{1,0:T(8,128)(2,1)S(1)}, bf16[64,128]{1,0:T(8,128)(2,1)S(1)}, u32[]{:S(2)}, u32[]{:S(2)}) collective-permute-start(bf16[64,128]{1,0:T(8,128)(2,1)S(1)} %get-tuple-element.33), channel_id=1, source_target_pairs={{0,2},{2,0},{4,6},{6,4},{8,10},{10,8},{12,14},{14,12},{16,18},{18,... | collective-permute-start | bytes 49160 | tf_op jit(solution)/shard_map/ppermute | solution.py:529
  17.9 1.4 %collective-permute-start.9 = (bf16[64,128]{1,0:T(8,128)(2,1)S(1)}, bf16[64,128]{1,0:T(8,128)(2,1)S(1)}, u32[]{:S(2)}, u32[]{:S(2)}) collective-permute-start(bf16[64,128]{1,0:T(8,128)(2,1)S(1)} %get-tuple-element.34), channel_id=1, source_target_pairs={{0,4},{2,6},{4,0},{6,2},{8,12},{10,14},{12,8},{14,10},{16,20},{18,... | collective-permute-start | bytes 49160 | tf_op jit(solution)/shard_map/ppermute | solution.py:529
  19.3 0.0 copy-done.2
  19.3 0.0 slice-done
  19.3 0.1 pad_maximum_fusion
  19.5 0.9 %collective-permute-done.7 = bf16[64,128]{1,0:T(8,128)(2,1)S(1)} collective-permute-done((bf16[64,128]{1,0:T(8,128)(2,1)S(1)}, bf16[64,128]{1,0:T(8,128)(2,1)S(1)}, u32[]{:S(2)}, u32[]{:S(2)}) %collective-permute-start.7) | collective-permute-done | bytes 16416 | tf_op jit(solution)/shard_map/ppermute | solution.py:529
  20.4 0.6 %collective-permute-done.8 = bf16[64,128]{1,0:T(8,128)(2,1)S(1)} collective-permute-done((bf16[64,128]{1,0:T(8,128)(2,1)S(1)}, bf16[64,128]{1,0:T(8,128)(2,1)S(1)}, u32[]{:S(2)}, u32[]{:S(2)}) %collective-permute-start.8) | collective-permute-done | bytes 16416 | tf_op jit(solution)/shard_map/ppermute | solution.py:529
  21.0 0.6 %collective-permute-done.9 = bf16[64,128]{1,0:T(8,128)(2,1)S(1)} collective-permute-done((bf16[64,128]{1,0:T(8,128)(2,1)S(1)}, bf16[64,128]{1,0:T(8,128)(2,1)S(1)}, u32[]{:S(2)}, u32[]{:S(2)}) %collective-permute-start.9) | collective-permute-done | bytes 16416 | tf_op jit(solution)/shard_map/ppermute | solution.py:529
  21.6 2.7 %collective-permute-start.10 = (bf16[4,64,128]{2,1,0:T(8,128)(2,1)S(1)}, bf16[4,64,128]{2,1,0:T(8,128)(2,1)S(1)}, u32[]{:S(2)}, u32[]{:S(2)}) collective-permute-start(bf16[4,64,128]{2,1,0:T(8,128)(2,1)S(1)} %pad_maximum_fusion.1.own), channel_id=1, source_target_pairs={{0,16},{2,18},{4,20},{6,22},{8,24},{10,26},{12,28},{14,30},{16,0},... | collective-permute-start | bytes 196616 | tf_op jit(solution)/shard_map/ppermute | solution.py:529
  24.3 0.4 %collective-permute-start.11 = (bf16[4,64,128]{2,1,0:T(8,128)(2,1)S(1)}, bf16[4,64,128]{2,1,0:T(8,128)(2,1)S(1)}, u32[]{:S(2)}, u32[]{:S(2)}) collective-permute-start(bf16[4,64,128]{2,1,0:T(8,128)(2,1)S(1)} %pad_maximum_fusion.1.own), channel_id=1, source_target_pairs={{0,8},{2,10},{4,12},{6,14},{8,0},{10,2},{12,4},{14,6},{16,24},{18,... | collective-permute-start | bytes 196616 | tf_op jit(solution)/shard_map/ppermute | solution.py:529
  24.7 2.3 %collective-permute-start.12 = (bf16[4,64,128]{2,1,0:T(8,128)(2,1)S(1)}, bf16[4,64,128]{2,1,0:T(8,128)(2,1)S(1)}, u32[]{:S(2)}, u32[]{:S(2)}) collective-permute-start(bf16[4,64,128]{2,1,0:T(8,128)(2,1)S(1)} %pad_maximum_fusion.1.own), channel_id=1, source_target_pairs={{8,16},{10,18},{12,20},{14,22},{16,8},{18,10},{20,12},{22,14},{9,1... | collective-permute-start | bytes 196616 | tf_op jit(solution)/shard_map/ppermute | solution.py:529
  27.1 0.3 collective-permute-done.10.far_c.far_d
  27.4 1.2 %collective-permute-done.11.near_a = bf16[4,64,128]{2,1,0:T(8,128)(2,1)S(1)} collective-permute-done((bf16[4,64,128]{2,1,0:T(8,128)(2,1)S(1)}, bf16[4,64,128]{2,1,0:T(8,128)(2,1)S(1)}, u32[]{:S(2)}, u32[]{:S(2)}) %collective-permute-start.11) | collective-permute-done | bytes 65568 | tf_op jit(solution)/shard_map/ppermute | solution.py:529
  28.6 2.3 %collective-permute-done.12.near_b = bf16[4,64,128]{2,1,0:T(8,128)(2,1)S(1)} collective-permute-done((bf16[4,64,128]{2,1,0:T(8,128)(2,1)S(1)}, bf16[4,64,128]{2,1,0:T(8,128)(2,1)S(1)}, u32[]{:S(2)}, u32[]{:S(2)}) %collective-permute-start.12) | collective-permute-done | bytes 65568 | tf_op jit(solution)/shard_map/ppermute | solution.py:529
  30.9 0.0 copy-done
  30.9 5.8 %shard_map.115 = (bf16[64,128]{1,0:T(8,128)(2,1)S(1)}, bf16[64,128]{1,0:T(8,128)(2,1)S(1)}, bf16[64,128]{1,0:T(8,128)(2,1)S(1)}, bf16[64,128]{1,0:T(8,128)(2,1)S(1)}) custom-call(bf16[4,64,128]{2,1,0:T(8,128)(2,1)S(1)} %pad_maximum_fusion.1.own, bf16[4,64,128]{2,1,0:T(8,128)(2,1)S(1)} %collective-permute-done.10.far_c.far_d, ...), custom_call_target="tpu_custom_call" | custom-call | tf_op jit(solution)/shard_map/pallas_call | solution.py:639
  36.7 0.9 %collective-permute-start.13 = (bf16[64,128]{1,0:T(8,128)(2,1)S(1)}, bf16[64,128]{1,0:T(8,128)(2,1)S(1)}, u32[]{:S(2)}, u32[]{:S(2)}) collective-permute-start(bf16[64,128]{1,0:T(8,128)(2,1)S(1)} %get-tuple-element.39), channel_id=1, source_target_pairs={{0,6},{2,4},{4,2},{6,0},{8,14},{10,12},{12,10},{14,8},{16,22},{18,... | collective-permute-start | bytes 49160 | tf_op jit(solution)/shard_map/ppermute | solution.py:529
  37.7 2.0 %collective-permute-start.14 = (bf16[64,128]{1,0:T(8,128)(2,1)S(1)}, bf16[64,128]{1,0:T(8,128)(2,1)S(1)}, u32[]{:S(2)}, u32[]{:S(2)}) collective-permute-start(bf16[64,128]{1,0:T(8,128)(2,1)S(1)} %get-tuple-element.40), channel_id=1, source_target_pairs={{0,2},{2,0},{4,6},{6,4},{8,10},{10,8},{12,14},{14,12},{16,18},{18,... | collective-permute-start | bytes 49160 | tf_op jit(solution)/shard_map/ppermute | solution.py:529
  39.7 0.6 %collective-permute-start.15 = (bf16[64,128]{1,0:T(8,128)(2,1)S(1)}, bf16[64,128]{1,0:T(8,128)(2,1)S(1)}, u32[]{:S(2)}, u32[]{:S(2)}) collective-permute-start(bf16[64,128]{1,0:T(8,128)(2,1)S(1)} %get-tuple-element.41), channel_id=1, source_target_pairs={{0,4},{2,6},{4,0},{6,2},{8,12},{10,14},{12,8},{14,10},{16,20},{18,... | collective-permute-start | bytes 49160 | tf_op jit(solution)/shard_map/ppermute | solution.py:529
  40.3 1.1 %collective-permute-done.13.from_1 = bf16[64,128]{1,0:T(8,128)(2,1)S(1)} collective-permute-done((bf16[64,128]{1,0:T(8,128)(2,1)S(1)}, bf16[64,128]{1,0:T(8,128)(2,1)S(1)}, u32[]{:S(2)}, u32[]{:S(2)}) %collective-permute-start.13) | collective-permute-done | bytes 16416 | tf_op jit(solution)/shard_map/ppermute | solution.py:529
  41.4 0.1 collective-permute-done.14.from_2
  41.6 1.9 %collective-permute-done.15.from_3 = bf16[64,128]{1,0:T(8,128)(2,1)S(1)} collective-permute-done((bf16[64,128]{1,0:T(8,128)(2,1)S(1)}, bf16[64,128]{1,0:T(8,128)(2,1)S(1)}, u32[]{:S(2)}, u32[]{:S(2)}) %collective-permute-start.15) | collective-permute-done | bytes 16416 | tf_op jit(solution)/shard_map/ppermute | solution.py:529
  43.4 0.6 %shard_map.116 = (f32[1,128]{1,0:T(1,128)}, bf16[1,128,128]{2,1,0:T(8,128)(2,1)}) custom-call(bf16[64,128]{1,0:T(8,128)(2,1)S(1)} %get-tuple-element.38.from_0, bf16[64,128]{1,0:T(8,128)(2,1)S(1)} %collective-permute-done.13.from_1, bf16[64,128]{1,0:T(8,128)(2,1)S(1)} %collective-permute-done.14.from_2, bf16[64,128]{1,0:T(8,128)(2,1)S(1)} %collective-permute-done.15.from_3), custom_call_target="tpu_custom_call" | custom-call | tf_op jit(solution)/shard_map/pallas_call | solution.py:662
  (3 shorter events, 0.1 us)
Async XLA Ops:
  0.6 5.6 %copy-start.1 = (bf16[1,128,128]{2,1,0:T(8,128)(2,1)S(1)}, bf16[1,128,128]{2,1,0:T(8,128)(2,1)}, u32[]{:S(2)}) copy-start(bf16[1,128,128]{2,1,0:T(8,128)(2,1)} %param.14) | copy-start | bytes 98308
  1.4 4.9 %collective-permute-start = (bf16[192,128]{1,0:T(8,128)(2,1)S(1)}, bf16[192,128]{1,0:T(8,128)(2,1)S(1)}, u32[]{:S(2)}, u32[]{:S(2)}) collective-permute-start(bf16[192,128]{1,0:T(8,128)(2,1)S(1)} %pad_maximum_fusion.2.own), channel_id=1, source_target_pairs={{0,1},{1,0},{2,3},{3,2},{4,5},{5,4},{6,7},{7,6},{8,9},{9,8},{10,11... | collective-permute-start | bytes 147464 | tf_op jit(solution)/shard_map/ppermute | solution.py:509
  1.4 6.9 %collective-permute-start.1 = (bf16[192,128]{1,0:T(8,128)(2,1)S(1)}, bf16[192,128]{1,0:T(8,128)(2,1)S(1)}, u32[]{:S(2)}, u32[]{:S(2)}) collective-permute-start(bf16[192,128]{1,0:T(8,128)(2,1)S(1)} %pad_maximum_fusion.2.own), channel_id=1, source_target_pairs={{0,2},{2,0},{4,6},{6,4},{8,10},{10,8},{12,14},{14,12},{16,18},{18,... | collective-permute-start | bytes 147464 | tf_op jit(solution)/shard_map/ppermute | solution.py:529
  3.0 7.8 %collective-permute-start.2 = (bf16[192,128]{1,0:T(8,128)(2,1)S(1)}, bf16[192,128]{1,0:T(8,128)(2,1)S(1)}, u32[]{:S(2)}, u32[]{:S(2)}) collective-permute-start(bf16[192,128]{1,0:T(8,128)(2,1)S(1)} %pad_maximum_fusion.2.own), channel_id=1, source_target_pairs={{2,4},{4,2},{6,8},{8,6},{10,12},{12,10},{14,16},{16,14},{18,20},{2... | collective-permute-start | bytes 147464 | tf_op jit(solution)/shard_map/ppermute | solution.py:529
  6.2 2.0 %collective-permute-start.3 = (bf16[128,128]{1,0:T(8,128)(2,1)S(1)}, bf16[128,128]{1,0:T(8,128)(2,1)S(1)}, u32[]{:S(2)}, u32[]{:S(2)}) collective-permute-start(bf16[128,128]{1,0:T(8,128)(2,1)S(1)} %bitcast.22), channel_id=1, source_target_pairs={{0,1},{1,0},{2,3},{3,2},{4,5},{5,4},{6,7},{7,6},{8,9},{9,8},{10,11... | collective-permute-start | bytes 98312 | tf_op jit(solution)/shard_map/ppermute | solution.py:509
  10.7 1.7 %collective-permute-start.4 = (bf16[192,128]{1,0:T(8,128)(2,1)S(1)}, bf16[192,128]{1,0:T(8,128)(2,1)S(1)}, u32[]{:S(2)}, u32[]{:S(2)}) collective-permute-start(bf16[192,128]{1,0:T(8,128)(2,1)S(1)} %collective-permute-done.1.odd_own), channel_id=1, source_target_pairs={{0,1},{1,0},{2,3},{3,2},{4,5},{5,4},{6,7},{7,6},{8,9},{9,8},{10,11... | collective-permute-start | bytes 147464 | tf_op jit(solution)/shard_map/ppermute | solution.py:509
  10.7 1.7 %collective-permute-start.5 = (bf16[192,128]{1,0:T(8,128)(2,1)S(1)}, bf16[192,128]{1,0:T(8,128)(2,1)S(1)}, u32[]{:S(2)}, u32[]{:S(2)}) collective-permute-start(bf16[192,128]{1,0:T(8,128)(2,1)S(1)} %collective-permute-done.2.even_own), channel_id=1, source_target_pairs={{0,1},{1,0},{2,3},{3,2},{4,5},{5,4},{6,7},{7,6},{8,9},{9,8},{10,11... | collective-permute-start | bytes 147464 | tf_op jit(solution)/shard_map/ppermute | solution.py:509
  11.2 1.2 %collective-permute-start.6 = (s32[8,128]{1,0:T(8,128)S(1)}, s32[8,128]{1,0:T(8,128)S(1)}, u32[]{:S(2)}, u32[]{:S(2)}) collective-permute-start(s32[8,128]{1,0:T(8,128)S(1)} %get-tuple-element.27.marks), channel_id=1, source_target_pairs={{0,1},{1,0},{2,3},{3,2},{4,5},{5,4},{6,7},{7,6},{8,9},{9,8},{10,11... | collective-permute-start | bytes 12296 | tf_op jit(solution)/shard_map/ppermute | solution.py:509
  12.4 6.9 %copy-start.2 = (bf16[3,3,9,384]{3,1,2,0:T(4,128)(2,1)S(1)}, bf16[3,3,9,384]{3,1,2,0:T(4,128)(2,1)}, u32[]{:S(2)}) copy-start(bf16[3,3,9,384]{3,1,2,0:T(4,128)(2,1)} %param.18) | copy-start | bytes 186628
  12.4 6.9 %slice-start = ((bf16[3,3,9,384]{3,1,2,0:T(4,128)(2,1)}), bf16[3,3,8,384]{3,1,2,0:T(4,128)(2,1)S(1)}, s32[]{:S(2)}) async-start(bf16[3,3,9,384]{3,1,2,0:T(4,128)(2,1)} %param.18), calls=%async_computation | async-start | bytes 147456 | tf_op jit(solution)/shard_map/slice | solution.py:599
  15.7 15.2 %copy-start = (bf16[3,3,128,384]{3,2,1,0:T(8,128)(2,1)S(1)}, bf16[3,3,128,384]{3,2,1,0:T(8,128)(2,1)}, u32[]{:S(2)}) copy-start(bf16[3,3,128,384]{3,2,1,0:T(8,128)(2,1)} %param.17) | copy-start | bytes 2654212
  15.7 4.7 %collective-permute-start.7 = (bf16[64,128]{1,0:T(8,128)(2,1)S(1)}, bf16[64,128]{1,0:T(8,128)(2,1)S(1)}, u32[]{:S(2)}, u32[]{:S(2)}) collective-permute-start(bf16[64,128]{1,0:T(8,128)(2,1)S(1)} %get-tuple-element.32), channel_id=1, source_target_pairs={{0,6},{2,4},{4,2},{6,0},{8,14},{10,12},{12,10},{14,8},{16,22},{18,... | collective-permute-start | bytes 49160 | tf_op jit(solution)/shard_map/ppermute | solution.py:529
  17.3 3.7 %collective-permute-start.8 = (bf16[64,128]{1,0:T(8,128)(2,1)S(1)}, bf16[64,128]{1,0:T(8,128)(2,1)S(1)}, u32[]{:S(2)}, u32[]{:S(2)}) collective-permute-start(bf16[64,128]{1,0:T(8,128)(2,1)S(1)} %get-tuple-element.33), channel_id=1, source_target_pairs={{0,2},{2,0},{4,6},{6,4},{8,10},{10,8},{12,14},{14,12},{16,18},{18,... | collective-permute-start | bytes 49160 | tf_op jit(solution)/shard_map/ppermute | solution.py:529
  17.9 3.7 %collective-permute-start.9 = (bf16[64,128]{1,0:T(8,128)(2,1)S(1)}, bf16[64,128]{1,0:T(8,128)(2,1)S(1)}, u32[]{:S(2)}, u32[]{:S(2)}) collective-permute-start(bf16[64,128]{1,0:T(8,128)(2,1)S(1)} %get-tuple-element.34), channel_id=1, source_target_pairs={{0,4},{2,6},{4,0},{6,2},{8,12},{10,14},{12,8},{14,10},{16,20},{18,... | collective-permute-start | bytes 49160 | tf_op jit(solution)/shard_map/ppermute | solution.py:529
  21.6 5.7 %collective-permute-start.10 = (bf16[4,64,128]{2,1,0:T(8,128)(2,1)S(1)}, bf16[4,64,128]{2,1,0:T(8,128)(2,1)S(1)}, u32[]{:S(2)}, u32[]{:S(2)}) collective-permute-start(bf16[4,64,128]{2,1,0:T(8,128)(2,1)S(1)} %pad_maximum_fusion.1.own), channel_id=1, source_target_pairs={{0,16},{2,18},{4,20},{6,22},{8,24},{10,26},{12,28},{14,30},{16,0},... | collective-permute-start | bytes 196616 | tf_op jit(solution)/shard_map/ppermute | solution.py:529
  24.3 4.3 %collective-permute-start.11 = (bf16[4,64,128]{2,1,0:T(8,128)(2,1)S(1)}, bf16[4,64,128]{2,1,0:T(8,128)(2,1)S(1)}, u32[]{:S(2)}, u32[]{:S(2)}) collective-permute-start(bf16[4,64,128]{2,1,0:T(8,128)(2,1)S(1)} %pad_maximum_fusion.1.own), channel_id=1, source_target_pairs={{0,8},{2,10},{4,12},{6,14},{8,0},{10,2},{12,4},{14,6},{16,24},{18,... | collective-permute-start | bytes 196616 | tf_op jit(solution)/shard_map/ppermute | solution.py:529
  24.7 6.1 %collective-permute-start.12 = (bf16[4,64,128]{2,1,0:T(8,128)(2,1)S(1)}, bf16[4,64,128]{2,1,0:T(8,128)(2,1)S(1)}, u32[]{:S(2)}, u32[]{:S(2)}) collective-permute-start(bf16[4,64,128]{2,1,0:T(8,128)(2,1)S(1)} %pad_maximum_fusion.1.own), channel_id=1, source_target_pairs={{8,16},{10,18},{12,20},{14,22},{16,8},{18,10},{20,12},{22,14},{9,1... | collective-permute-start | bytes 196616 | tf_op jit(solution)/shard_map/ppermute | solution.py:529
  36.7 4.7 %collective-permute-start.13 = (bf16[64,128]{1,0:T(8,128)(2,1)S(1)}, bf16[64,128]{1,0:T(8,128)(2,1)S(1)}, u32[]{:S(2)}, u32[]{:S(2)}) collective-permute-start(bf16[64,128]{1,0:T(8,128)(2,1)S(1)} %get-tuple-element.39), channel_id=1, source_target_pairs={{0,6},{2,4},{4,2},{6,0},{8,14},{10,12},{12,10},{14,8},{16,22},{18,... | collective-permute-start | bytes 49160 | tf_op jit(solution)/shard_map/ppermute | solution.py:529
  37.7 3.9 %collective-permute-start.14 = (bf16[64,128]{1,0:T(8,128)(2,1)S(1)}, bf16[64,128]{1,0:T(8,128)(2,1)S(1)}, u32[]{:S(2)}, u32[]{:S(2)}) collective-permute-start(bf16[64,128]{1,0:T(8,128)(2,1)S(1)} %get-tuple-element.40), channel_id=1, source_target_pairs={{0,2},{2,0},{4,6},{6,4},{8,10},{10,8},{12,14},{14,12},{16,18},{18,... | collective-permute-start | bytes 49160 | tf_op jit(solution)/shard_map/ppermute | solution.py:529
  39.7 3.7 %collective-permute-start.15 = (bf16[64,128]{1,0:T(8,128)(2,1)S(1)}, bf16[64,128]{1,0:T(8,128)(2,1)S(1)}, u32[]{:S(2)}, u32[]{:S(2)}) collective-permute-start(bf16[64,128]{1,0:T(8,128)(2,1)S(1)} %get-tuple-element.41), channel_id=1, source_target_pairs={{0,4},{2,6},{4,0},{6,2},{8,12},{10,14},{12,8},{14,10},{16,20},{18,... | collective-permute-start | bytes 49160 | tf_op jit(solution)/shard_map/ppermute | solution.py:529

commit v2 on v1

--- a/solution.py
+++ b/solution.py
@@ -95,6 +95,10 @@
     return stacked.reshape(values[0].shape[0] * len(values), values[0].shape[1])
 
 
+def toeplitz_kernel(vol_kernel, out):
+    out[...] = toeplitz(vol_kernel)
+
+
 def correlate(lefts, rights, place, row_ok, wide, extra):
     has_left = (place[1] > 0).astype(f32)
     has_right = (place[1] < place[3] - 1).astype(f32)
@@ -154,8 +158,8 @@
 
 
 def own_row_kernel(
-    own, across, limit, indices, gain, head, vol_kernel, raw_out, taps_out, marks_out, gains_out,
-    heads_out, wide, extra, limits, index_rows, gain_held, head_held, kernel, sems,
+    own, across, limit, indices, gain, head, vol_kernel, raw_out, kernel_out, marks_out,
+    gains_out, heads_out, wide, extra, limits, index_rows, gain_held, head_held, kernel, sems,
 ):
     place = position()
     copies = [
@@ -188,11 +192,11 @@
     gains_out[...] = gains
     heads = head_held[...].astype(f32) * feature_scale
     heads_out[...] = jnp.broadcast_to(heads, heads_out.shape).astype(bf16)
-    taps_out[...] = toeplitz(kernel)
+    kernel_out[...] = kernel[...]
 
 
 def volume_kernel(
-    gains, odd_own, odd_across, even_own, even_across, marks, marks_across, hidden,
+    gains, even_own, even_across, odd_own, odd_across, marks, marks_across, hidden,
     hidden_across, raw_own, taps_own, out_0, out_1, out_2, out_3, raw, taps, wide, extra, logit, padded, blocks, sems,
 ):
     place = position()
@@ -558,13 +562,13 @@
     padded = (DISPS + 2) * GROUPS
 
     feats = jnp.concatenate([feat_left[0], feat_right[0]], axis=0)
-    odd_own, even_own = to_rows(feats, odd_pair), to_rows(feats, even_pair)
+    even_own, odd_own = to_rows(feats, even_pair), to_rows(feats, odd_pair)
     across = to_sides(feats)
-    raw_own, taps, marks, gains, heads = pl.pallas_call(
+    raw_own, kernel_held, marks, gains, heads = pl.pallas_call(
         own_row_kernel,
         out_shape=(
             jax.ShapeDtypeStruct((padded, 2 * TILE), bf16),
-            jax.ShapeDtypeStruct((3 * OUT_SLAB, 3 * SLAB), bf16),
+            jax.ShapeDtypeStruct((27, GROUPS, GROUPS), bf16),
             jax.ShapeDtypeStruct((GROUPS, TILE), jnp.int32),
             jax.ShapeDtypeStruct((GROUPS, TILE), f32),
             jax.ShapeDtypeStruct((HID_CH, HID_CH), bf16),
@@ -589,11 +593,19 @@
     )
     hidden = hidden_start[0]
     hidden_across = to_sides(hidden)
-    odd_own, even_own, raw_own, taps, hidden_across = lax.optimization_barrier(
-        (odd_own, even_own, raw_own, taps, hidden_across)
-    )
+    even_own, odd_own, raw_own, hidden_across = lax.optimization_barrier(
+        (even_own, odd_own, raw_own, hidden_across)
+    )
+    taps = pl.pallas_call(
+        toeplitz_kernel,
+        out_shape=jax.ShapeDtypeStruct((3 * OUT_SLAB, 3 * SLAB), bf16),
+        in_specs=[vmem],
+        out_specs=vmem,
+        compiler_params=pltpu.CompilerParams(vmem_limit_bytes=8 * 2**20),
+        cost_estimate=pl.CostEstimate(flops=10**9, bytes_accessed=2**20, transcendentals=0),
+    )(kernel_held)
     marks_across = to_sides(marks)
-    odd_across, even_across = to_sides(odd_own), to_sides(even_own)
+    even_across, odd_across = to_sides(even_own), to_sides(odd_own)
 
     in_weight = jnp.concatenate(
         [in_kernel[:, :, :GROUPS]] * ITERS + [in_kernel[:, :, GROUPS:]], axis=2
@@ -621,7 +633,7 @@
             flops=5 * 10**9, bytes_accessed=16 * 2**20, transcendentals=DISPS * TILE
         ),
     )(
-        gains, odd_own, odd_across, even_own, even_across,
+        gains, even_own, even_across, odd_own, odd_across,
         marks, marks_across, hidden, hidden_across, raw_own, taps,
     )
 

time: 44.3 us -> 43.4 us (0.980)
  waiting for transfers between devices: 12.6 us -> 11.7 us
    ppermute x11, waiting for transfers between devices: 11.5 us -> 10.7 us  [to_rows(): lax.ppermute(value, 'band', [(i, shift(i)) for i in range(bands) if 0 <=...]
  transfers between devices with their start and end apart: 16 -> 16, of which waited for: 11 -> 12; matrix products, arithmetic and copies ran while one was open for 0% -> 0% of each run, Pallas kernels for 4% -> 5%
where the time goes in v2:
time: 43.4 us; the launch traced here: 43.1 us
  starting transfers between devices  18 us (41%)
  waiting for transfers between devices  11.7 us (27%)
  Pallas kernels  11.7 us (27%)
  other arithmetic  0.9 us (2%)
  between operations  0.75 us (2%)
    ppermute x11, starting transfers between devices, to_rows(): lax.ppermute(value, 'band', [(i, shift(i)) for i in range(bands) if 0 <=...  17.5 us
    ppermute x11, waiting for transfers between devices, to_rows(): lax.ppermute(value, 'band', [(i, shift(i)) for i in range(bands) if 0 <=...  10.7 us
    pallas_call x1, Pallas kernels, local(): pl.pallas_call(refine_kernel, out_shape=(jax.ShapeDtypeStruct((2 * STRIP,...  5.83 us
    pallas_call x1, Pallas kernels, local(): pl.pallas_call(volume_kernel, out_shape=(jax.ShapeDtypeStruct((BLOCK_ROWS...  3.29 us
    pallas_call x1, Pallas kernels, local(): pl.pallas_call(own_row_kernel, out_shape=(jax.ShapeDtypeStruct((padded, 2...  1.71 us
    ppermute x5, waiting for transfers between devices, to_sides(): return lax.ppermute(value, 'disp', right + left)[None]  0.93 us
  transfers between devices with their start and end apart: 16, of which 12 were waited for; matrix products, arithmetic and copies ran while one was open for 0% of the time, Pallas kernels for 5%

profile of v2, /device:TPU:8, one launch (start us, length us, event | category | flops | bytes accessed | tf_op | source)
XLA Modules:
  0.0 43.1 jit_solution(2404144229823283192)
XLA Ops:
  0.6 0.0 copy-start.1
  0.6 0.8 %pad_maximum_fusion.2.own = bf16[192,128]{1,0:T(8,128)(2,1)S(1)} fusion(bf16[96,128]{1,0:T(8,128)(2,1)} %bitcast.26, bf16[96,128]{1,0:T(8,128)(2,1)} %bitcast.27), kind=kLoop, calls=%fused_computation.2 | loop fusion | flops 98304 | bytes 98304 | tf_op jit(solution)/shard_map/concatenate | solution.py:564
  1.4 0.0 collective-permute-start
  1.4 4.2 %collective-permute-start.1 = (bf16[192,128]{1,0:T(8,128)(2,1)S(1)}, bf16[192,128]{1,0:T(8,128)(2,1)S(1)}, u32[]{:S(2)}, u32[]{:S(2)}) collective-permute-start(bf16[192,128]{1,0:T(8,128)(2,1)S(1)} %pad_maximum_fusion.2.own), channel_id=1, source_target_pairs={{2,4},{4,2},{6,8},{8,6},{10,12},{12,10},{14,16},{16,14},{18,20},{2... | collective-permute-start | bytes 147464 | tf_op jit(solution)/shard_map/ppermute | solution.py:533
  5.6 0.7 %collective-permute-start.2 = (bf16[192,128]{1,0:T(8,128)(2,1)S(1)}, bf16[192,128]{1,0:T(8,128)(2,1)S(1)}, u32[]{:S(2)}, u32[]{:S(2)}) collective-permute-start(bf16[192,128]{1,0:T(8,128)(2,1)S(1)} %pad_maximum_fusion.2.own), channel_id=1, source_target_pairs={{0,2},{2,0},{4,6},{6,4},{8,10},{10,8},{12,14},{14,12},{16,18},{18,... | collective-permute-start | bytes 147464 | tf_op jit(solution)/shard_map/ppermute | solution.py:533
  6.4 0.0 copy-done.1
  6.4 0.0 collective-permute-start.3
  6.4 0.0 collective-permute-done
  6.4 1.7 %shard_map.113 = (bf16[784,256]{1,0:T(8,128)(2,1)S(1)}, bf16[27,8,8]{2,1,0:T(8,128)(2,1)S(1)}, s32[8,128]{1,0:T(8,128)S(1)}, f32[8,128]{1,0:T(8,128)S(1)}, bf16[128,128]{1,0:T(8,128)(2,1)S(1)}) custom-call(bf16[192,128]{1,0:T(8,128)(2,1)S(1)} %pad_maximum_fusion.2.own, bf16[1,192,128]{2,1,0:T(8,128)(2,1)S(1)} %bitcast.21, s32[1,128]{1,0:T(1,128)} %limit.1, ...), custom_call_target="tpu_custom_call" | custom-call | flops 2000000000 | bytes 4194304 | tf_op jit(solution)/shard_map/pallas_call | solution.py:567
  8.1 0.0 collective-permute-done.3
  8.1 1.2 %collective-permute-done.1.even_own = bf16[192,128]{1,0:T(8,128)(2,1)S(1)} collective-permute-done((bf16[192,128]{1,0:T(8,128)(2,1)S(1)}, bf16[192,128]{1,0:T(8,128)(2,1)S(1)}, u32[]{:S(2)}, u32[]{:S(2)}) %collective-permute-start.1) | collective-permute-done | bytes 49184 | tf_op jit(solution)/shard_map/ppermute | solution.py:533
  9.3 0.5 %collective-permute-done.2.odd_own = bf16[192,128]{1,0:T(8,128)(2,1)S(1)} collective-permute-done((bf16[192,128]{1,0:T(8,128)(2,1)S(1)}, bf16[192,128]{1,0:T(8,128)(2,1)S(1)}, u32[]{:S(2)}, u32[]{:S(2)}) %collective-permute-start.2) | collective-permute-done | bytes 49184 | tf_op jit(solution)/shard_map/ppermute | solution.py:533
  9.8 0.0 collective-permute-start.4
  9.8 0.5 %collective-permute-start.5 = (bf16[192,128]{1,0:T(8,128)(2,1)S(1)}, bf16[192,128]{1,0:T(8,128)(2,1)S(1)}, u32[]{:S(2)}, u32[]{:S(2)}) collective-permute-start(bf16[192,128]{1,0:T(8,128)(2,1)S(1)} %collective-permute-done.2.odd_own), channel_id=1, source_target_pairs={{0,1},{1,0},{2,3},{3,2},{4,5},{5,4},{6,7},{7,6},{8,9},{9,8},{10,11... | collective-permute-start | bytes 147464 | tf_op jit(solution)/shard_map/ppermute | solution.py:513
  10.3 0.0 collective-permute-start.6
  10.3 0.2 shard_map.114.taps_own
  10.6 0.9 %collective-permute-done.6 = s32[8,128]{1,0:T(8,128)S(1)} collective-permute-done((s32[8,128]{1,0:T(8,128)S(1)}, s32[8,128]{1,0:T(8,128)S(1)}, u32[]{:S(2)}, u32[]{:S(2)}) %collective-permute-start.6) | collective-permute-done | bytes 4128 | tf_op jit(solution)/shard_map/ppermute | solution.py:513
  11.5 0.0 collective-permute-done.4
  11.5 0.0 collective-permute-done.5
  11.5 0.0 copy-start.2
  11.5 0.0 slice-start
  11.5 3.3 %shard_map.115 = (bf16[64,128]{1,0:T(8,128)(2,1)S(1)}, bf16[64,128]{1,0:T(8,128)(2,1)S(1)}, bf16[64,128]{1,0:T(8,128)(2,1)S(1)}, bf16[64,128]{1,0:T(8,128)(2,1)S(1)}) custom-call(f32[8,128]{1,0:T(8,128)S(1)} %get-tuple-element.21.gains, bf16[192,128]{1,0:T(8,128)(2,1)S(1)} %collective-permute-done.1.even_own, bf16[1,192,128]{2,1,0:T(8,128)(2,1)S(1)} %bitcast.19, ...), custom_call_target="tpu_custom_call" | custom-call | flops 5000000000 | bytes 16777216 | tf_op jit(solution)/shard_map/pallas_call | solution.py:616
  14.8 0.0 copy-start
  14.8 2.0 %collective-permute-start.7 = (bf16[64,128]{1,0:T(8,128)(2,1)S(1)}, bf16[64,128]{1,0:T(8,128)(2,1)S(1)}, u32[]{:S(2)}, u32[]{:S(2)}) collective-permute-start(bf16[64,128]{1,0:T(8,128)(2,1)S(1)} %get-tuple-element.30), channel_id=1, source_target_pairs={{0,6},{2,4},{4,2},{6,0},{8,14},{10,12},{12,10},{14,8},{16,22},{18,... | collective-permute-start | bytes 49160 | tf_op jit(solution)/shard_map/ppermute | solution.py:533
  16.9 0.5 %collective-permute-start.8 = (bf16[64,128]{1,0:T(8,128)(2,1)S(1)}, bf16[64,128]{1,0:T(8,128)(2,1)S(1)}, u32[]{:S(2)}, u32[]{:S(2)}) collective-permute-start(bf16[64,128]{1,0:T(8,128)(2,1)S(1)} %get-tuple-element.31), channel_id=1, source_target_pairs={{0,2},{2,0},{4,6},{6,4},{8,10},{10,8},{12,14},{14,12},{16,18},{18,... | collective-permute-start | bytes 49160 | tf_op jit(solution)/shard_map/ppermute | solution.py:533
  17.4 1.0 %collective-permute-start.9 = (bf16[64,128]{1,0:T(8,128)(2,1)S(1)}, bf16[64,128]{1,0:T(8,128)(2,1)S(1)}, u32[]{:S(2)}, u32[]{:S(2)}) collective-permute-start(bf16[64,128]{1,0:T(8,128)(2,1)S(1)} %get-tuple-element.32), channel_id=1, source_target_pairs={{0,4},{2,6},{4,0},{6,2},{8,12},{10,14},{12,8},{14,10},{16,20},{18,... | collective-permute-start | bytes 49160 | tf_op jit(solution)/shard_map/ppermute | solution.py:533
  18.4 0.0 copy-done.2
  18.4 0.0 slice-done
  18.4 0.1 pad_maximum_fusion
  18.6 0.9 %collective-permute-done.7 = bf16[64,128]{1,0:T(8,128)(2,1)S(1)} collective-permute-done((bf16[64,128]{1,0:T(8,128)(2,1)S(1)}, bf16[64,128]{1,0:T(8,128)(2,1)S(1)}, u32[]{:S(2)}, u32[]{:S(2)}) %collective-permute-start.7) | collective-permute-done | bytes 16416 | tf_op jit(solution)/shard_map/ppermute | solution.py:533
  19.5 1.1 %collective-permute-done.8 = bf16[64,128]{1,0:T(8,128)(2,1)S(1)} collective-permute-done((bf16[64,128]{1,0:T(8,128)(2,1)S(1)}, bf16[64,128]{1,0:T(8,128)(2,1)S(1)}, u32[]{:S(2)}, u32[]{:S(2)}) %collective-permute-start.8) | collective-permute-done | bytes 16416 | tf_op jit(solution)/shard_map/ppermute | solution.py:533
  20.6 0.5 %collective-permute-done.9 = bf16[64,128]{1,0:T(8,128)(2,1)S(1)} collective-permute-done((bf16[64,128]{1,0:T(8,128)(2,1)S(1)}, bf16[64,128]{1,0:T(8,128)(2,1)S(1)}, u32[]{:S(2)}, u32[]{:S(2)}) %collective-permute-start.9) | collective-permute-done | bytes 16416 | tf_op jit(solution)/shard_map/ppermute | solution.py:533
  21.2 2.7 %collective-permute-start.10 = (bf16[4,64,128]{2,1,0:T(8,128)(2,1)S(1)}, bf16[4,64,128]{2,1,0:T(8,128)(2,1)S(1)}, u32[]{:S(2)}, u32[]{:S(2)}) collective-permute-start(bf16[4,64,128]{2,1,0:T(8,128)(2,1)S(1)} %pad_maximum_fusion.1.own), channel_id=1, source_target_pairs={{0,16},{2,18},{4,20},{6,22},{8,24},{10,26},{12,28},{14,30},{16,0},... | collective-permute-start | bytes 196616 | tf_op jit(solution)/shard_map/ppermute | solution.py:533
  23.8 0.4 %collective-permute-start.11 = (bf16[4,64,128]{2,1,0:T(8,128)(2,1)S(1)}, bf16[4,64,128]{2,1,0:T(8,128)(2,1)S(1)}, u32[]{:S(2)}, u32[]{:S(2)}) collective-permute-start(bf16[4,64,128]{2,1,0:T(8,128)(2,1)S(1)} %pad_maximum_fusion.1.own), channel_id=1, source_target_pairs={{0,8},{2,10},{4,12},{6,14},{8,0},{10,2},{12,4},{14,6},{16,24},{18,... | collective-permute-start | bytes 196616 | tf_op jit(solution)/shard_map/ppermute | solution.py:533
  24.3 2.3 %collective-permute-start.12 = (bf16[4,64,128]{2,1,0:T(8,128)(2,1)S(1)}, bf16[4,64,128]{2,1,0:T(8,128)(2,1)S(1)}, u32[]{:S(2)}, u32[]{:S(2)}) collective-permute-start(bf16[4,64,128]{2,1,0:T(8,128)(2,1)S(1)} %pad_maximum_fusion.1.own), channel_id=1, source_target_pairs={{8,16},{10,18},{12,20},{14,22},{16,8},{18,10},{20,12},{22,14},{9,1... | collective-permute-start | bytes 196616 | tf_op jit(solution)/shard_map/ppermute | solution.py:533
  26.6 0.3 collective-permute-done.10.far_c.far_d
  26.9 1.2 %collective-permute-done.11.near_a = bf16[4,64,128]{2,1,0:T(8,128)(2,1)S(1)} collective-permute-done((bf16[4,64,128]{2,1,0:T(8,128)(2,1)S(1)}, bf16[4,64,128]{2,1,0:T(8,128)(2,1)S(1)}, u32[]{:S(2)}, u32[]{:S(2)}) %collective-permute-start.11) | collective-permute-done | bytes 65568 | tf_op jit(solution)/shard_map/ppermute | solution.py:533
  28.1 2.3 %collective-permute-done.12.near_b = bf16[4,64,128]{2,1,0:T(8,128)(2,1)S(1)} collective-permute-done((bf16[4,64,128]{2,1,0:T(8,128)(2,1)S(1)}, bf16[4,64,128]{2,1,0:T(8,128)(2,1)S(1)}, u32[]{:S(2)}, u32[]{:S(2)}) %collective-permute-start.12) | collective-permute-done | bytes 65568 | tf_op jit(solution)/shard_map/ppermute | solution.py:533
  30.4 0.0 copy-done
  30.4 5.8 %shard_map.116 = (bf16[64,128]{1,0:T(8,128)(2,1)S(1)}, bf16[64,128]{1,0:T(8,128)(2,1)S(1)}, bf16[64,128]{1,0:T(8,128)(2,1)S(1)}, bf16[64,128]{1,0:T(8,128)(2,1)S(1)}) custom-call(bf16[4,64,128]{2,1,0:T(8,128)(2,1)S(1)} %pad_maximum_fusion.1.own, bf16[4,64,128]{2,1,0:T(8,128)(2,1)S(1)} %collective-permute-done.10.far_c.far_d, ...), custom_call_target="tpu_custom_call" | custom-call | tf_op jit(solution)/shard_map/pallas_call | solution.py:651
  36.2 2.0 %collective-permute-start.13 = (bf16[64,128]{1,0:T(8,128)(2,1)S(1)}, bf16[64,128]{1,0:T(8,128)(2,1)S(1)}, u32[]{:S(2)}, u32[]{:S(2)}) collective-permute-start(bf16[64,128]{1,0:T(8,128)(2,1)S(1)} %get-tuple-element.37), channel_id=1, source_target_pairs={{0,6},{2,4},{4,2},{6,0},{8,14},{10,12},{12,10},{14,8},{16,22},{18,... | collective-permute-start | bytes 49160 | tf_op jit(solution)/shard_map/ppermute | solution.py:533
  38.2 0.5 %collective-permute-start.14 = (bf16[64,128]{1,0:T(8,128)(2,1)S(1)}, bf16[64,128]{1,0:T(8,128)(2,1)S(1)}, u32[]{:S(2)}, u32[]{:S(2)}) collective-permute-start(bf16[64,128]{1,0:T(8,128)(2,1)S(1)} %get-tuple-element.38), channel_id=1, source_target_pairs={{0,2},{2,0},{4,6},{6,4},{8,10},{10,8},{12,14},{14,12},{16,18},{18,... | collective-permute-start | bytes 49160 | tf_op jit(solution)/shard_map/ppermute | solution.py:533
  38.8 1.1 %collective-permute-start.15 = (bf16[64,128]{1,0:T(8,128)(2,1)S(1)}, bf16[64,128]{1,0:T(8,128)(2,1)S(1)}, u32[]{:S(2)}, u32[]{:S(2)}) collective-permute-start(bf16[64,128]{1,0:T(8,128)(2,1)S(1)} %get-tuple-element.39), channel_id=1, source_target_pairs={{0,4},{2,6},{4,0},{6,2},{8,12},{10,14},{12,8},{14,10},{16,20},{18,... | collective-permute-start | bytes 49160 | tf_op jit(solution)/shard_map/ppermute | solution.py:533
  39.8 1.1 %collective-permute-done.13.from_1 = bf16[64,128]{1,0:T(8,128)(2,1)S(1)} collective-permute-done((bf16[64,128]{1,0:T(8,128)(2,1)S(1)}, bf16[64,128]{1,0:T(8,128)(2,1)S(1)}, u32[]{:S(2)}, u32[]{:S(2)}) %collective-permute-start.13) | collective-permute-done | bytes 16416 | tf_op jit(solution)/shard_map/ppermute | solution.py:533
  41.0 1.0 %collective-permute-done.14.from_2 = bf16[64,128]{1,0:T(8,128)(2,1)S(1)} collective-permute-done((bf16[64,128]{1,0:T(8,128)(2,1)S(1)}, bf16[64,128]{1,0:T(8,128)(2,1)S(1)}, u32[]{:S(2)}, u32[]{:S(2)}) %collective-permute-start.14) | collective-permute-done | bytes 16416 | tf_op jit(solution)/shard_map/ppermute | solution.py:533
  42.0 0.5 %collective-permute-done.15.from_3 = bf16[64,128]{1,0:T(8,128)(2,1)S(1)} collective-permute-done((bf16[64,128]{1,0:T(8,128)(2,1)S(1)}, bf16[64,128]{1,0:T(8,128)(2,1)S(1)}, u32[]{:S(2)}, u32[]{:S(2)}) %collective-permute-start.15) | collective-permute-done | bytes 16416 | tf_op jit(solution)/shard_map/ppermute | solution.py:533
  42.5 0.6 %shard_map.117 = (f32[1,128]{1,0:T(1,128)}, bf16[1,128,128]{2,1,0:T(8,128)(2,1)}) custom-call(bf16[64,128]{1,0:T(8,128)(2,1)S(1)} %get-tuple-element.36.from_0, bf16[64,128]{1,0:T(8,128)(2,1)S(1)} %collective-permute-done.13.from_1, bf16[64,128]{1,0:T(8,128)(2,1)S(1)} %collective-permute-done.14.from_2, bf16[64,128]{1,0:T(8,128)(2,1)S(1)} %collective-permute-done.15.from_3), custom_call_target="tpu_custom_call" | custom-call | tf_op jit(solution)/shard_map/pallas_call | solution.py:674
  (3 shorter events, 0.1 us)
Async XLA Ops:
  0.6 5.7 %copy-start.1 = (bf16[1,128,128]{2,1,0:T(8,128)(2,1)S(1)}, bf16[1,128,128]{2,1,0:T(8,128)(2,1)}, u32[]{:S(2)}) copy-start(bf16[1,128,128]{2,1,0:T(8,128)(2,1)} %param.14) | copy-start | bytes 98308
  1.4 5.0 %collective-permute-start = (bf16[192,128]{1,0:T(8,128)(2,1)S(1)}, bf16[192,128]{1,0:T(8,128)(2,1)S(1)}, u32[]{:S(2)}, u32[]{:S(2)}) collective-permute-start(bf16[192,128]{1,0:T(8,128)(2,1)S(1)} %pad_maximum_fusion.2.own), channel_id=1, source_target_pairs={{0,1},{1,0},{2,3},{3,2},{4,5},{5,4},{6,7},{7,6},{8,9},{9,8},{10,11... | collective-permute-start | bytes 147464 | tf_op jit(solution)/shard_map/ppermute | solution.py:513
  1.4 7.9 %collective-permute-start.1 = (bf16[192,128]{1,0:T(8,128)(2,1)S(1)}, bf16[192,128]{1,0:T(8,128)(2,1)S(1)}, u32[]{:S(2)}, u32[]{:S(2)}) collective-permute-start(bf16[192,128]{1,0:T(8,128)(2,1)S(1)} %pad_maximum_fusion.2.own), channel_id=1, source_target_pairs={{2,4},{4,2},{6,8},{8,6},{10,12},{12,10},{14,16},{16,14},{18,20},{2... | collective-permute-start | bytes 147464 | tf_op jit(solution)/shard_map/ppermute | solution.py:533
  5.6 4.2 %collective-permute-start.2 = (bf16[192,128]{1,0:T(8,128)(2,1)S(1)}, bf16[192,128]{1,0:T(8,128)(2,1)S(1)}, u32[]{:S(2)}, u32[]{:S(2)}) collective-permute-start(bf16[192,128]{1,0:T(8,128)(2,1)S(1)} %pad_maximum_fusion.2.own), channel_id=1, source_target_pairs={{0,2},{2,0},{4,6},{6,4},{8,10},{10,8},{12,14},{14,12},{16,18},{18,... | collective-permute-start | bytes 147464 | tf_op jit(solution)/shard_map/ppermute | solution.py:533
  6.4 1.7 %collective-permute-start.3 = (bf16[128,128]{1,0:T(8,128)(2,1)S(1)}, bf16[128,128]{1,0:T(8,128)(2,1)S(1)}, u32[]{:S(2)}, u32[]{:S(2)}) collective-permute-start(bf16[128,128]{1,0:T(8,128)(2,1)S(1)} %bitcast.22), channel_id=1, source_target_pairs={{0,1},{1,0},{2,3},{3,2},{4,5},{5,4},{6,7},{7,6},{8,9},{9,8},{10,11... | collective-permute-start | bytes 98312 | tf_op jit(solution)/shard_map/ppermute | solution.py:513
  9.8 1.7 %collective-permute-start.4 = (bf16[192,128]{1,0:T(8,128)(2,1)S(1)}, bf16[192,128]{1,0:T(8,128)(2,1)S(1)}, u32[]{:S(2)}, u32[]{:S(2)}) collective-permute-start(bf16[192,128]{1,0:T(8,128)(2,1)S(1)} %collective-permute-done.1.even_own), channel_id=1, source_target_pairs={{0,1},{1,0},{2,3},{3,2},{4,5},{5,4},{6,7},{7,6},{8,9},{9,8},{10,11... | collective-permute-start | bytes 147464 | tf_op jit(solution)/shard_map/ppermute | solution.py:513
  9.8 1.7 %collective-permute-start.5 = (bf16[192,128]{1,0:T(8,128)(2,1)S(1)}, bf16[192,128]{1,0:T(8,128)(2,1)S(1)}, u32[]{:S(2)}, u32[]{:S(2)}) collective-permute-start(bf16[192,128]{1,0:T(8,128)(2,1)S(1)} %collective-permute-done.2.odd_own), channel_id=1, source_target_pairs={{0,1},{1,0},{2,3},{3,2},{4,5},{5,4},{6,7},{7,6},{8,9},{9,8},{10,11... | collective-permute-start | bytes 147464 | tf_op jit(solution)/shard_map/ppermute | solution.py:513
  10.3 1.2 %collective-permute-start.6 = (s32[8,128]{1,0:T(8,128)S(1)}, s32[8,128]{1,0:T(8,128)S(1)}, u32[]{:S(2)}, u32[]{:S(2)}) collective-permute-start(s32[8,128]{1,0:T(8,128)S(1)} %get-tuple-element.25.marks), channel_id=1, source_target_pairs={{0,1},{1,0},{2,3},{3,2},{4,5},{5,4},{6,7},{7,6},{8,9},{9,8},{10,11... | collective-permute-start | bytes 12296 | tf_op jit(solution)/shard_map/ppermute | solution.py:513
  11.5 6.9 %copy-start.2 = (bf16[3,3,9,384]{3,1,2,0:T(4,128)(2,1)S(1)}, bf16[3,3,9,384]{3,1,2,0:T(4,128)(2,1)}, u32[]{:S(2)}) copy-start(bf16[3,3,9,384]{3,1,2,0:T(4,128)(2,1)} %param.18) | copy-start | bytes 186628
  11.5 6.9 %slice-start = ((bf16[3,3,9,384]{3,1,2,0:T(4,128)(2,1)}), bf16[3,3,8,384]{3,1,2,0:T(4,128)(2,1)S(1)}, s32[]{:S(2)}) async-start(bf16[3,3,9,384]{3,1,2,0:T(4,128)(2,1)} %param.18), calls=%async_computation | async-start | bytes 147456 | tf_op jit(solution)/shard_map/slice | solution.py:611
  14.8 15.6 %copy-start = (bf16[3,3,128,384]{3,2,1,0:T(8,128)(2,1)S(1)}, bf16[3,3,128,384]{3,2,1,0:T(8,128)(2,1)}, u32[]{:S(2)}) copy-start(bf16[3,3,128,384]{3,2,1,0:T(8,128)(2,1)} %param.17) | copy-start | bytes 2654212
  14.8 4.7 %collective-permute-start.7 = (bf16[64,128]{1,0:T(8,128)(2,1)S(1)}, bf16[64,128]{1,0:T(8,128)(2,1)S(1)}, u32[]{:S(2)}, u32[]{:S(2)}) collective-permute-start(bf16[64,128]{1,0:T(8,128)(2,1)S(1)} %get-tuple-element.30), channel_id=1, source_target_pairs={{0,6},{2,4},{4,2},{6,0},{8,14},{10,12},{12,10},{14,8},{16,22},{18,... | collective-permute-start | bytes 49160 | tf_op jit(solution)/shard_map/ppermute | solution.py:533
  16.9 3.7 %collective-permute-start.8 = (bf16[64,128]{1,0:T(8,128)(2,1)S(1)}, bf16[64,128]{1,0:T(8,128)(2,1)S(1)}, u32[]{:S(2)}, u32[]{:S(2)}) collective-permute-start(bf16[64,128]{1,0:T(8,128)(2,1)S(1)} %get-tuple-element.31), channel_id=1, source_target_pairs={{0,2},{2,0},{4,6},{6,4},{8,10},{10,8},{12,14},{14,12},{16,18},{18,... | collective-permute-start | bytes 49160 | tf_op jit(solution)/shard_map/ppermute | solution.py:533
  17.4 3.7 %collective-permute-start.9 = (bf16[64,128]{1,0:T(8,128)(2,1)S(1)}, bf16[64,128]{1,0:T(8,128)(2,1)S(1)}, u32[]{:S(2)}, u32[]{:S(2)}) collective-permute-start(bf16[64,128]{1,0:T(8,128)(2,1)S(1)} %get-tuple-element.32), channel_id=1, source_target_pairs={{0,4},{2,6},{4,0},{6,2},{8,12},{10,14},{12,8},{14,10},{16,20},{18,... | collective-permute-start | bytes 49160 | tf_op jit(solution)/shard_map/ppermute | solution.py:533
  21.2 5.7 %collective-permute-start.10 = (bf16[4,64,128]{2,1,0:T(8,128)(2,1)S(1)}, bf16[4,64,128]{2,1,0:T(8,128)(2,1)S(1)}, u32[]{:S(2)}, u32[]{:S(2)}) collective-permute-start(bf16[4,64,128]{2,1,0:T(8,128)(2,1)S(1)} %pad_maximum_fusion.1.own), channel_id=1, source_target_pairs={{0,16},{2,18},{4,20},{6,22},{8,24},{10,26},{12,28},{14,30},{16,0},... | collective-permute-start | bytes 196616 | tf_op jit(solution)/shard_map/ppermute | solution.py:533
  23.8 4.3 %collective-permute-start.11 = (bf16[4,64,128]{2,1,0:T(8,128)(2,1)S(1)}, bf16[4,64,128]{2,1,0:T(8,128)(2,1)S(1)}, u32[]{:S(2)}, u32[]{:S(2)}) collective-permute-start(bf16[4,64,128]{2,1,0:T(8,128)(2,1)S(1)} %pad_maximum_fusion.1.own), channel_id=1, source_target_pairs={{0,8},{2,10},{4,12},{6,14},{8,0},{10,2},{12,4},{14,6},{16,24},{18,... | collective-permute-start | bytes 196616 | tf_op jit(solution)/shard_map/ppermute | solution.py:533
  24.3 6.1 %collective-permute-start.12 = (bf16[4,64,128]{2,1,0:T(8,128)(2,1)S(1)}, bf16[4,64,128]{2,1,0:T(8,128)(2,1)S(1)}, u32[]{:S(2)}, u32[]{:S(2)}) collective-permute-start(bf16[4,64,128]{2,1,0:T(8,128)(2,1)S(1)} %pad_maximum_fusion.1.own), channel_id=1, source_target_pairs={{8,16},{10,18},{12,20},{14,22},{16,8},{18,10},{20,12},{22,14},{9,1... | collective-permute-start | bytes 196616 | tf_op jit(solution)/shard_map/ppermute | solution.py:533
  36.2 4.7 %collective-permute-start.13 = (bf16[64,128]{1,0:T(8,128)(2,1)S(1)}, bf16[64,128]{1,0:T(8,128)(2,1)S(1)}, u32[]{:S(2)}, u32[]{:S(2)}) collective-permute-start(bf16[64,128]{1,0:T(8,128)(2,1)S(1)} %get-tuple-element.37), channel_id=1, source_target_pairs={{0,6},{2,4},{4,2},{6,0},{8,14},{10,12},{12,10},{14,8},{16,22},{18,... | collective-permute-start | bytes 49160 | tf_op jit(solution)/shard_map/ppermute | solution.py:533
  38.2 3.7 %collective-permute-start.14 = (bf16[64,128]{1,0:T(8,128)(2,1)S(1)}, bf16[64,128]{1,0:T(8,128)(2,1)S(1)}, u32[]{:S(2)}, u32[]{:S(2)}) collective-permute-start(bf16[64,128]{1,0:T(8,128)(2,1)S(1)} %get-tuple-element.38), channel_id=1, source_target_pairs={{0,2},{2,0},{4,6},{6,4},{8,10},{10,8},{12,14},{14,12},{16,18},{18,... | collective-permute-start | bytes 49160 | tf_op jit(solution)/shard_map/ppermute | solution.py:533
  38.8 3.7 %collective-permute-start.15 = (bf16[64,128]{1,0:T(8,128)(2,1)S(1)}, bf16[64,128]{1,0:T(8,128)(2,1)S(1)}, u32[]{:S(2)}, u32[]{:S(2)}) collective-permute-start(bf16[64,128]{1,0:T(8,128)(2,1)S(1)} %get-tuple-element.39), channel_id=1, source_target_pairs={{0,4},{2,6},{4,0},{6,2},{8,12},{10,14},{12,8},{14,10},{16,20},{18,... | collective-permute-start | bytes 49160 | tf_op jit(solution)/shard_map/ppermute | solution.py:533
